TPU v7x, 256 devices: a whole 4x4x8 slice. The times are simulated.
256 devices in a mesh: seq: 16 (over y, x_hi, core), grp: 16 (over x_lo, z).
Axes of the slice: x: 4 (x_hi: 2, x_lo: 2; x = x_hi * 2 + x_lo), y: 4, z: 8, core: 2. Of those that a mesh axis runs over, the one named last changes fastest.
Arguments:
- video_qkv: bfloat16 [3, 2048, 2048], P(None, 'seq', 'grp'), may hold values from -13 to 13
- audio_qkv: bfloat16 [3, 1024, 2048], P(None, 'seq', 'grp'), may hold values from -13 to 13
- head_slopes: float32 [16], P('grp'), may hold values from 0.05 to 0.8
- audio_frame: int32 [1024], replicated, may hold values from 0 to 31, as said below
- out_weight: bfloat16 [2048, 3072], P('grp'), may hold values from -0.125 to 0.125
- video_cot: bfloat16 [2048, 3072], P('seq', 'grp'), may hold values from -6 to 6
- audio_cot: bfloat16 [1024, 2048], P('seq', 'grp'), may hold values from -6 to 6
Outputs:
- video_out: bfloat16 [2048, 3072], P('seq', 'grp')
- audio_mix: bfloat16 [1024, 2048], P('seq', 'grp')
- video_grad: bfloat16 [3, 2048, 2048], P(None, 'seq', 'grp')
- audio_grad: bfloat16 [3, 1024, 2048], P(None, 'seq', 'grp')
Inputs may be any that keep to these rules, and one draw needn't show every extreme that they name: `audio_frame`: audio token a lies within two frames of frame a * 32 // 1024; the first audio token lies in frame 0 and the last in frame 32 - 1.
All inputs are finite; a program needn't handle non-finite values.
Results may differ from a plain program's by a relative error of at most 0.035.
Values may be sent and summed in bfloat16 or wider, within the bound.
A program may use at most 64 MiB of HBM per device.

v0:
```python
import math

import jax
import jax.numpy as jnp
from jax import lax
from jax.sharding import PartitionSpec as P


def block_size(amount):
    if amount <= 1024:
        return amount
    return math.gcd(amount, 1024)


def pair_scores(queries, key_part, query_frame, key_frame, slope_rate, scaling):
    scores = (
        jnp.einsum("qd,kd->qk", queries, key_part, preferred_element_type=jnp.float32) * scaling
    )
    if slope_rate is None:
        return scores
    return scores - slope_rate * jnp.abs(query_frame[:, None] - key_frame[None, :]).astype(
        jnp.float32
    )


def split_keys(key_part, value_part, frames):
    amount, head_width = key_part.shape
    size_each = block_size(amount)
    number = amount // size_each
    return (
        key_part.reshape(number, size_each, head_width),
        value_part.reshape(number, size_each, head_width),
        frames.reshape(number, size_each),
    )


def softmax_norm(queries, query_frame, key_sets, scaling):
    row_count = queries.shape[0]
    running_state = (
        jnp.full((row_count,), -1e30, jnp.float32),
        jnp.zeros((row_count,), jnp.float32),
    )
    for key_part, value_part, frames, slope_rate in key_sets:

        def softmax_update(running, pieces):
            highest, summed = running
            scores = pair_scores(queries, pieces[0], query_frame, pieces[2], slope_rate, scaling)
            new_high = jnp.maximum(highest, jnp.max(scores, axis=1))
            summed = summed * jnp.exp(highest - new_high) + jnp.sum(
                jnp.exp(scores - new_high[:, None]), axis=1
            )
            return ((new_high, summed), None)

        running_state, unused = lax.scan(
            softmax_update, running_state, split_keys(key_part, value_part, frames)
        )
    return running_state[0] + jnp.log(running_state[1])


def attend(queries, query_frame, key_sets, log_norm, scaling):
    mixed_rows = jnp.zeros(queries.shape, jnp.float32)
    for key_part, value_part, frames, slope_rate in key_sets:

        def attend_update(running, pieces):
            scores = pair_scores(queries, pieces[0], query_frame, pieces[2], slope_rate, scaling)
            weights = jnp.exp(scores - log_norm[:, None]).astype(jnp.bfloat16)
            return (
                running
                + jnp.einsum("qk,kd->qd", weights, pieces[1], preferred_element_type=jnp.float32),
                None,
            )

        mixed_rows, unused = lax.scan(
            attend_update, mixed_rows, split_keys(key_part, value_part, frames)
        )
    return mixed_rows.astype(jnp.bfloat16)


def query_gradient(queries, query_frame, key_sets, grad_out, out_dot, log_norm, scaling):
    summed = jnp.zeros(queries.shape, jnp.float32)
    for key_part, value_part, frames, slope_rate in key_sets:

        def query_update(running, pieces):
            scores = pair_scores(queries, pieces[0], query_frame, pieces[2], slope_rate, scaling)
            probable = jnp.exp(scores - log_norm[:, None])
            prob_grad = jnp.einsum(
                "qd,kd->qk", grad_out, pieces[1], preferred_element_type=jnp.float32
            )
            score_grad = (probable * (prob_grad - out_dot[:, None])).astype(jnp.bfloat16)
            return (
                running
                + jnp.einsum(
                    "qk,kd->qd", score_grad, pieces[0], preferred_element_type=jnp.float32
                ),
                None,
            )

        summed, unused = lax.scan(query_update, summed, split_keys(key_part, value_part, frames))
    return (summed * scaling).astype(jnp.bfloat16)


def key_gradient(
    key_part,
    value_part,
    key_frame,
    queries,
    query_frame,
    grad_out,
    out_dot,
    log_norm,
    slope_rate,
    scaling,
):
    row_count, head_width = queries.shape
    size_each = block_size(row_count)
    number = row_count // size_each
    query_blocks = (
        queries.reshape(number, size_each, head_width),
        query_frame.reshape(number, size_each),
        grad_out.reshape(number, size_each, head_width),
        out_dot.reshape(number, size_each),
        log_norm.reshape(number, size_each),
    )

    def one_block(key_pieces):
        block_keys, block_values, block_frames = key_pieces

        def one_update(running, pieces):
            block_queries, block_qframe, block_grads, block_dot, block_norm = pieces
            scores = pair_scores(
                block_queries, block_keys, block_qframe, block_frames, slope_rate, scaling
            )
            probable = jnp.exp(scores - block_norm[:, None])
            prob_grad = jnp.einsum(
                "qd,kd->qk", block_grads, block_values, preferred_element_type=jnp.float32
            )
            score_grad = (probable * (prob_grad - block_dot[:, None])).astype(jnp.bfloat16)
            key_sum = running[0] + jnp.einsum(
                "qk,qd->kd", score_grad, block_queries, preferred_element_type=jnp.float32
            )
            value_sum = running[1] + jnp.einsum(
                "qk,qd->kd",
                probable.astype(jnp.bfloat16),
                block_grads,
                preferred_element_type=jnp.float32,
            )
            return ((key_sum, value_sum), None)

        zeros_block = jnp.zeros(block_keys.shape, jnp.float32)
        (key_sum, value_sum), unused = lax.scan(
            one_update, (zeros_block, zeros_block), query_blocks
        )
        return jnp.concatenate([key_sum * scaling, value_sum], axis=1)

    result = lax.map(one_block, split_keys(key_part, value_part, key_frame))
    return result.reshape(key_part.shape[0], 2 * head_width)


def per_device(video_qkv, audio_qkv, head_slopes, audio_frame, out_weight, video_cot, audio_cot):
    head_width = video_qkv.shape[2]
    video_rows = video_qkv.shape[1]
    audio_rows = audio_qkv.shape[1]
    scaling = head_width ** (-0.5)
    seq_count = lax.axis_size("seq")
    seq_index = lax.axis_index("seq")
    video_kv, audio_kv = (
        lax.all_gather(video_qkv[1:], "seq", axis=1, tiled=True),
        lax.all_gather(audio_qkv[1:], "seq", axis=1, tiled=True),
    )
    cot_full = lax.all_gather(video_cot, "grp", axis=1, tiled=True)
    video_frame = jnp.arange(video_rows * seq_count, dtype=jnp.int32) // (video_rows // 2)
    own_frame = lax.dynamic_slice_in_dim(video_frame, seq_index * video_rows, video_rows)
    audio_own_frame = lax.dynamic_slice_in_dim(audio_frame, seq_index * audio_rows, audio_rows)
    slope_rate = head_slopes[0]
    video_side = (
        (video_kv[0], video_kv[1], video_frame, None),
        (audio_kv[0], audio_kv[1], audio_frame, slope_rate),
    )
    audio_side = (
        (video_kv[0], video_kv[1], video_frame, slope_rate),
        (audio_kv[0], audio_kv[1], audio_frame, None),
    )
    video_query = video_qkv[0]
    audio_query = audio_qkv[0]
    video_norm = softmax_norm(video_query, own_frame, video_side, scaling)
    video_mix = attend(video_query, own_frame, video_side, video_norm, scaling)
    audio_norm = softmax_norm(audio_query, audio_own_frame, audio_side, scaling)
    audio_mix = attend(audio_query, audio_own_frame, audio_side, audio_norm, scaling)
    projected = jnp.dot(video_mix, out_weight, preferred_element_type=jnp.float32)
    video_out = lax.psum_scatter(
        projected.astype(jnp.bfloat16), "grp", scatter_dimension=1, tiled=True
    )
    grad_video = jnp.einsum(
        "te,he->th", cot_full, out_weight, preferred_element_type=jnp.float32
    ).astype(jnp.bfloat16)
    video_dot = jnp.sum(grad_video.astype(jnp.float32) * video_mix.astype(jnp.float32), axis=1)
    audio_dot = jnp.sum(audio_cot.astype(jnp.float32) * audio_mix.astype(jnp.float32), axis=1)
    video_dq = query_gradient(
        video_query, own_frame, video_side, grad_video, video_dot, video_norm, scaling
    )
    audio_dq = query_gradient(
        audio_query, audio_own_frame, audio_side, audio_cot, audio_dot, audio_norm, scaling
    )
    per_block = video_rows + audio_rows
    block_count = (video_rows + audio_rows) * lax.axis_size("seq") // per_block
    video_part = key_gradient(
        video_kv[0],
        video_kv[1],
        video_frame,
        video_query,
        own_frame,
        grad_video,
        video_dot,
        video_norm,
        None,
        scaling,
    )
    video_part = video_part + key_gradient(
        video_kv[0],
        video_kv[1],
        video_frame,
        audio_query,
        audio_own_frame,
        audio_cot,
        audio_dot,
        audio_norm,
        slope_rate,
        scaling,
    )
    audio_part = key_gradient(
        audio_kv[0],
        audio_kv[1],
        audio_frame,
        video_query,
        own_frame,
        grad_video,
        video_dot,
        video_norm,
        slope_rate,
        scaling,
    )
    audio_part = audio_part + key_gradient(
        audio_kv[0],
        audio_kv[1],
        audio_frame,
        audio_query,
        audio_own_frame,
        audio_cot,
        audio_dot,
        audio_norm,
        None,
        scaling,
    )
    joined = jnp.concatenate(
        [
            video_part.reshape(block_count, video_rows, 2 * head_width),
            audio_part.reshape(block_count, audio_rows, 2 * head_width),
        ],
        axis=1,
    )
    key_terms = lax.psum_scatter(
        joined.reshape((video_rows + audio_rows) * lax.axis_size("seq"), 2 * head_width).astype(
            jnp.bfloat16
        ),
        "seq",
        scatter_dimension=0,
        tiled=True,
    ).astype(jnp.float32)
    video_terms = key_terms[:video_rows]
    audio_terms = key_terms[video_rows:]
    video_grad = jnp.stack(
        [
            video_dq,
            video_terms[:, :head_width].astype(jnp.bfloat16),
            video_terms[:, head_width:].astype(jnp.bfloat16),
        ]
    )
    audio_grad = jnp.stack(
        [
            audio_dq,
            audio_terms[:, :head_width].astype(jnp.bfloat16),
            audio_terms[:, head_width:].astype(jnp.bfloat16),
        ]
    )
    return (video_out, audio_mix, video_grad, audio_grad)


def solution(mesh):
    in_specs = (
        P(None, "seq", "grp"),
        P(None, "seq", "grp"),
        P("grp"),
        P(),
        P("grp", None),
        P("seq", "grp"),
        P("seq", "grp"),
    )
    out_specs = (P("seq", "grp"), P("seq", "grp"), P(None, "seq", "grp"), P(None, "seq", "grp"))
    return jax.shard_map(
        per_device, mesh=mesh, in_specs=in_specs, out_specs=out_specs, check_vma=False
    )
```

profile of v0, /device:TPU:16, one launch (start us, length us, event | category | flops | bytes accessed | tf_op | source)
XLA Modules:
  0.0 270.7 jit_solution(4365402910274354881)
XLA Ops:
  7.3 1.5 slice.58
  9.6 41.1 %all_gather.11 = bf16[128,3072]{0,1:T(8,128)(2,1)S(1)} all-gather(bf16[128,192]{0,1:T(8,128)(2,1)} %param.28), channel_id=1, replica_groups=mesh['seq'=16,'grp'=16] {'grp'}, dimensions={1}, use_global_device_ids=true | all-gather | bytes 835584 | tf_op jit(solution)/shard_map/all_gather | solution.py:170
  52.0 22.1 %all_gather.10 = bf16[2,1024,128]{2,1,0:T(8,128)(2,1)S(1)} all-gather(bf16[2,64,128]{2,1,0:T(8,128)(2,1)S(1)} %slice-done), channel_id=1, replica_groups=mesh['seq'=16,'grp'=16] {'seq'}, dimensions={1}, use_global_device_ids=true | all-gather | bytes 557056 | tf_op jit(solution)/shard_map/all_gather | solution.py:168
  74.8 2.1 fusion.182
  76.9 2.5 while.76
  81.0 4.3 %while.77 = (s32[]{:T(128)}, f32[64,128]{1,0:T(8,128)S(1)}, bf16[2,1024,128]{2,1,0:T(8,128)(2,1)S(1)}, bf16[64,128]{1,0:T(8,128)(2,1)S(1)}, f32[]{:T(128)}, /*in...) while((s32[]{:T(128)}, f32[64,128]{1,0:T(8,128)S(1)}, ...), condition=%wide.region_16.17_spmd.clone, body=%wide.region_15.16_spmd.clone.sunk | while | flops 34095104 | bytes 621698 | solution.py:73
  81.0 2.1 fusion.289
  83.1 2.1 fusion.289
  89.3 4.1 %while.70 = (s32[]{:T(128)}, f32[128,128]{1,0:T(8,128)}, bf16[2,1024,128]{2,1,0:T(8,128)(2,1)S(1)}, bf16[128,128]{1,0:T(8,128)(2,1)S(1)}, f32[128]{0:T(128)S(1)}...) while((s32[]{:T(128)}, f32[128,128]{1,0:T(8,128)}, ...), condition=%wide.region_7.8_spmd.clone, body=%wide.region_6.7_spmd.clone.sunk | while | flops 67534848 | bytes 690278 | solution.py:73
  89.3 2.1 fusion.281
  91.3 2.1 fusion.281
  96.0 1.3 fusion.160
  98.4 1.5 broadcast.158.clone2
  99.9 5.8 %while.33 = (s32[]{:T(128)}, f32[2,1024,256]{2,1,0:T(8,128)}, bf16[2,1024,128]{2,1,0:T(8,128)(2,1)S(1)}, bf16[1,128,128]{2,1,0:T(8,128)(2,1)S(1)}, f32[1,128]{1,...) while((s32[]{:T(128)}, f32[2,1024,256]{2,1,0:T(8,128)}, ...), condition=%wide.region_21.22_spmd, body=%wide.region_20.21_spmd.sunk | while | flops 135397376 | bytes 5375089 | solution.py:155
  100.1 1.4 convolution_multiply_fusion.16
  103.0 1.4 convolution_multiply_fusion.16
  105.6 1.5 broadcast.158.clone2.1
  107.1 8.1 %while.68 = (s32[]{:T(128)}, f32[2,1024,256]{2,1,0:T(8,128)}, bf16[2,1024,128]{2,1,0:T(8,128)(2,1)S(1)}, bf16[1,64,128]{2,1,0:T(8,128)(2,1)S(1)}, f32[]{:T(128)}...) while((s32[]{:T(128)}, f32[2,1024,256]{2,1,0:T(8,128)}, ...), condition=%wide.region_24.25_spmd, body=%wide.region_23.24_spmd.sunk | while | flops 68222976 | bytes 8733165 | solution.py:155
  108.0 1.3 convolution_multiply_fusion.17
  112.0 1.3 convolution_multiply_fusion.17
  115.1 2.5 add_convert_fusion
  117.7 1.3 pad_maximum_fusion
  119.2 4.8 %while.79 = (s32[]{:T(128)}, f32[64,128]{1,0:T(8,128)S(1)}, bf16[2,1024,128]{2,1,0:T(8,128)(2,1)S(1)}, bf16[64,128]{1,0:T(8,128)(2,1)S(1)}, f32[]{:T(128)}, /*in...) while((s32[]{:T(128)}, f32[64,128]{1,0:T(8,128)S(1)}, ...), condition=%wide.region_27.28_spmd.clone, body=%wide.region_26.27_spmd.clone.sunk | while | flops 51003392 | bytes 1423770 | solution.py:98
  119.2 1.2 fusion.301
  120.5 1.2 fusion.302
  122.8 1.2 fusion.302
  124.2 1.3 convolution_convert_fusion
  125.6 3.5 %while.78 = (s32[]{:T(128)}, f32[128,128]{1,0:T(8,128)S(1)}, bf16[2,1024,128]{2,1,0:T(8,128)(2,1)S(1)}, bf16[128,128]{1,0:T(8,128)(2,1)S(1)}, f32[128]{0:T(128)S...) while((s32[]{:T(128)}, f32[128,128]{1,0:T(8,128)S(1)}, ...), condition=%wide.region_19.20_spmd.clone, body=%wide.region_18.19_spmd.clone.sunk | while | flops 101351424 | bytes 2034298 | solution.py:98
  125.6 1.2 convolution_subtract_fusion.7
  127.4 1.2 convolution_subtract_fusion.7
  129.3 60.0 %reduce-scatter.5.cloned.1.call-done = bf16[192,256]{1,0:T(8,128)(2,1)} async-done(((bf16[3072,256]{1,0:T(8,128)(2,1)}), bf16[192,256]{1,0:T(8,128)(2,1)}) %reduce-scatter.5.cloned.1.call-update) | async-done | bytes 98320 | tf_op jit(solution)/shard_map/reduce_scatter | solution.py:261
  192.2 72.0 %reduce-scatter.3.cloned.1.call-done = bf16[128,192]{0,1:T(8,128)(2,1)} async-done(((bf16[128,3072]{0,1:T(8,128)(2,1)}), bf16[128,192]{0,1:T(8,128)(2,1)}) %reduce-scatter.3.cloned.1.call-update) | async-done | bytes 49168 | tf_op jit(solution)/shard_map/reduce_scatter | solution.py:190
  (152 shorter events, 28.4 us)
Async XLA Ops:
  7.2 43.6 %copy-start = (bf16[128,3072]{1,0:T(8,128)(2,1)S(1)}, bf16[128,3072]{1,0:T(8,128)(2,1)}, u32[]{:S(2)}) copy-start(bf16[128,3072]{1,0:T(8,128)(2,1)} %param.27) | copy-start | bytes 2359300
  7.2 44.8 %copy-start.9 = (bf16[3,128,128]{2,1,0:T(8,128)(2,1)S(1)}, bf16[3,128,128]{2,1,0:T(8,128)(2,1)}, u32[]{:S(2)}) copy-start(bf16[3,128,128]{2,1,0:T(8,128)(2,1)} %param.23) | copy-start | bytes 294916
  7.2 44.8 %copy-start.10 = (bf16[3,64,128]{2,1,0:T(8,128)(2,1)S(1)}, bf16[3,64,128]{2,1,0:T(8,128)(2,1)}, u32[]{:S(2)}) copy-start(bf16[3,64,128]{2,1,0:T(8,128)(2,1)} %param.24) | copy-start | bytes 147460
  7.2 44.8 %slice-start = ((bf16[3,64,128]{2,1,0:T(8,128)(2,1)}), bf16[2,64,128]{2,1,0:T(8,128)(2,1)S(1)}, s32[]{:S(2)}) async-start(bf16[3,64,128]{2,1,0:T(8,128)(2,1)} %param.24), calls=%async_computation.5 | async-start | bytes 65536 | tf_op jit(solution)/shard_map/slice | solution.py:168
  7.2 44.0 %copy-start.19 = (s32[1024]{0:T(1024)S(1)}, s32[1024]{0:T(1024)}, u32[]{:S(2)}) copy-start(s32[1024]{0:T(1024)} %param.26) | copy-start | bytes 12292
  7.2 67.6 %all-gather.2.cloned.1.call-start = ((), (), s32[]{:S(2)}) async-start(), calls=%async_computation.2 | async-start | bytes 1114112 | tf_op jit(solution)/shard_map/all_gather | solution.py:167
  8.8 180.5 %reduce-scatter.5.cloned.1.call-start = ((), (), s32[]{:S(2)}) async-start(), calls=%async_computation.4 | async-start | bytes 1671168 | tf_op jit(solution)/shard_map/reduce_scatter | solution.py:261
  74.1 20.6 %copy-start.1 = (bf16[2,1024,128]{2,1,0:T(8,128)(2,1)}, bf16[2,1024,128]{2,1,0:T(8,128)(2,1)S(1)}, u32[]{:S(2)}) copy-start(bf16[2,1024,128]{2,1,0:T(8,128)(2,1)S(1)} %all_gather.10) | copy-start | bytes 1572868
  80.4 0.6 copy-start.13
  81.0 4.3 %copy-start.3 = (bf16[64,128]{1,0:T(8,128)(2,1)S(1)}, bf16[64,128]{1,0:T(8,128)(2,1)}, u32[]{:S(2)}) copy-start(bf16[64,128]{1,0:T(8,128)(2,1)} %param.29) | copy-start | bytes 49156
  85.3 1.3 copy-start.15
  85.3 1.3 copy-start.20
  85.3 2.8 %copy-start.14 = (f32[128]{0:T(128)S(1)}, f32[128]{0:T(128)}, u32[]{:S(2)}) copy-start(f32[128]{0:T(128)} %copy-done.13) | copy-start | bytes 1540
  86.8 2.5 copy-start.7
  94.9 3.4 %copy-start.4 = (bf16[128,1024]{1,0:T(8,128)(2,1)}, bf16[128,1024]{1,0:T(8,128)(2,1)S(1)}, u32[]{:S(2)}) copy-start(bf16[128,1024]{1,0:T(8,128)(2,1)S(1)} %fusion.149) | copy-start | bytes 786436
  105.6 1.5 copy-start.11
  105.6 1.5 copy-start.22
  107.1 2.2 copy-start.17
  110.0 1.1 copy-start.18
  110.0 1.1 copy-start.23
  111.1 2.2 copy-start.17
  114.0 1.1 copy-start.18
  114.1 1.1 copy-start.23
  115.1 2.5 copy-start.6
  117.7 1.5 copy-start.16
  117.7 1.5 copy-start.21
  119.0 145.2 %reduce-scatter.3.cloned.1.call-start = ((), (), s32[]{:S(2)}) async-start(), calls=%async_computation.3 | async-start | bytes 835584 | tf_op jit(solution)/shard_map/reduce_scatter | solution.py:190
  119.2 4.8 %copy-start.2 = (bf16[2,1024,128]{2,1,0:T(8,128)(2,1)S(1)}, bf16[2,1024,128]{2,1,0:T(8,128)(2,1)}, u32[]{:S(2)}) copy-start(bf16[2,1024,128]{2,1,0:T(8,128)(2,1)} %copy-done.1) | copy-start | bytes 1572868
  119.2 4.8 %copy-start.8 = (bf16[64,1024]{1,0:T(8,128)(2,1)S(1)}, bf16[64,1024]{1,0:T(8,128)(2,1)}, u32[]{:S(2)}) copy-start(bf16[64,1024]{1,0:T(8,128)(2,1)} %copy-done.7) | copy-start | bytes 393220
  124.0 1.6 copy-start.12
  125.6 3.5 %copy-start.5 = (bf16[128,1024]{1,0:T(8,128)(2,1)S(1)}, bf16[128,1024]{1,0:T(8,128)(2,1)}, u32[]{:S(2)}) copy-start(bf16[128,1024]{1,0:T(8,128)(2,1)} %copy-done.4) | copy-start | bytes 786436
Sparse Core Ops, SparseCore 0:
  10.8 51.4 all-gather.1
  119.1 70.2 reduce-scatter.4
  192.6 71.4 reduce-scatter.2
where the time goes:
time: 272 us; the launch traced here: 271 us
  waiting for transfers between devices  132 us (49%)
  blocking collectives  63.2 us (23%)
  matrix products  35.6 us (13%)
  between operations  14.9 us (5%)
  local copies, waits for them, and re-layouts  14.2 us (5%)
  other arithmetic  10 us (4%)
    reduce_scatter x1, waiting for transfers between devices, per_device(): lax.psum_scatter(projected.astype(jnp.bfloat16), 'grp', scatter_dimension...  72 us
    reduce_scatter x1, waiting for transfers between devices, per_device(): lax.psum_scatter(joined.reshape((video_rows + audio_rows) * lax.axis_size...  60 us
    all_gather x1, blocking collectives, per_device(): cot_full = lax.all_gather(video_cot, 'grp', axis=1, tiled=True)  41.1 us
    all_gather x1, blocking collectives, per_device(): lax.all_gather(audio_qkv[1:], 'seq', axis=1, tiled=True)  22.1 us
    dot_general x6, matrix products, attend_update(): jnp.einsum('qk,kd->qd', weights, pieces[1], preferred_element_type=jnp.fl...  9.64 us
    dot_general x6, matrix products, one_update(): jnp.einsum('qk,qd->kd', score_grad, block_queries, preferred_element_type...  7.5 us
  transfers between devices with their start and end apart: 3, of which 2 were waited for; matrix products, arithmetic and copies ran while one was open for 5% of the time, Pallas kernels for 0%

commit v1 on v0

v1 whole, which is shorter than its diff:
```python
import math

import jax
import jax.numpy as jnp
from jax import lax
from jax.experimental import pallas as pl
from jax.experimental.pallas import tpu as pltpu
from jax.sharding import PartitionSpec as P

BF = jnp.bfloat16
F32 = jnp.float32
HD = 128
TV = 128
TA = 64
TT = TV + TA
NY = 4
NX = 4
NZ = 8
QV = NX * TV
QA = NX * TA
QT = QV + QA
COLS = 192
HALF = NZ * COLS
LOG2E = 1.4426950408889634

NN = (((1,), (0,)), ((), ()))
NT = (((1,), (1,)), ((), ()))


def mm(a, b, dims=NN):
    return lax.dot_general(a, b, dims, preferred_element_type=F32)


def roll64(x):
    return pltpu.roll(x, 64, 1)


def low_half(rows):
    return lax.broadcasted_iota(jnp.int32, (rows, 128), 1) < 64


def kernel(
    vqkv, aqkv, slope_ref, frame_ref, w_hbm, cot_hbm, acot_hbm,
    out_ref, amix_ref, vgrad_ref, agrad_ref,
    kv, q, gb, cotb, cot_raw, w, wp, wsend, bias_v, bias_a, p_scr,
    osend, orecv, st_send, st_recv, col_scr, mix_own, mix_par,
    gp_send, gp_recv, g_send, dot_buf, os, orx,
    dkv_send, dkv_recv, dkv_own, dq_send, dq_recv,
    lsem, ssem, rsem,
):
    s = lax.axis_index("seq")
    grp = lax.axis_index("grp")
    y = lax.div(s, NX)
    xc = lax.rem(s, NX)
    x_lo = lax.div(grp, NZ)
    z = lax.rem(grp, NZ)
    core = lax.rem(xc, 2)
    sibling = (s + 1 - 2 * core, grp)
    cross = (s, lax.rem(grp + NZ, 2 * NZ))

    def y_peer(k):
        return (lax.rem(s + NX * k, NX * NY), grp)

    def x_slot(k):
        return lax.rem(xc + k, NX)

    def x_peer(k):
        return (y * NX + x_slot(k), grp)

    def z_slot(k):
        return lax.rem(z + k, NZ)

    def z_peer(k):
        return (s, x_lo * NZ + z_slot(k))

    sends = []
    count = [0]

    def remote(src, dst, to):
        i = count[0]
        count[0] += 1
        copy = pltpu.make_async_remote_copy(
            src_ref=src,
            dst_ref=dst,
            send_sem=ssem.at[i],
            recv_sem=rsem.at[i],
            device_id=to,
            device_id_type=pl.DeviceIdType.MESH,
        )
        copy.start()
        sends.append(copy)
        return copy

    local_count = [0]

    def local(src, dst):
        i = local_count[0]
        local_count[0] += 1
        copy = pltpu.make_async_copy(src, dst, lsem.at[i])
        copy.start()
        return copy

    barrier = pltpu.get_barrier_semaphore()
    peers = (
        [z_peer(k) for k in range(1, NZ)]
        + [cross]
        + [y_peer(k) for k in range(1, NY)]
        + [x_peer(k) for k in range(1, NX)]
    )
    for peer in peers:
        pl.semaphore_signal(barrier, inc=1, device_id=peer, device_id_type=pl.DeviceIdType.MESH)

    xv = pl.ds(pl.multiple_of(xc * TV, TV), TV)
    xa = pl.ds(pl.multiple_of(QV + xc * TA, TA), TA)
    l_cot = local(cot_hbm, cot_raw)
    l_w = local(w_hbm, w)
    l_kvv = local(vqkv.at[1:3], kv.at[:, y, 0:TV])
    l_kva = local(aqkv.at[1:3], kv.at[:, y, TV:TT])
    l_qv = local(vqkv.at[0], q.at[xv])
    l_qa = local(aqkv.at[0], q.at[xa])
    l_ga = local(acot_hbm, gb.at[xa])

    l_cot.wait()
    lane_r = lax.broadcasted_iota(jnp.int32, (64, 128), 0)
    lane_c = lax.broadcasted_iota(jnp.int32, (64, 128), 1)
    place_lo = (lane_r == lane_c).astype(BF)
    place_hi = (lane_r + 64 == lane_c).astype(BF)
    tail = cot_raw[:, 128:192]
    cotb[z, 0:128, :] = cot_raw[:, 0:128]
    cotb[z, 128:192, :] = (mm(tail[0:64], place_lo) + mm(tail[64:128], place_hi)).astype(BF)

    pl.semaphore_wait(barrier, len(peers))

    r_cot = [remote(cotb.at[z], cotb.at[z], z_peer(k)) for k in (4, 3, 5, 2, 6, 1, 7)]
    r_kv, r_q, r_ga = [], [], []
    for k in (2, 1, 3):
        r_kv.append(remote(vqkv.at[1:3], kv.at[:, y, 0:TV], y_peer(k)))
        r_kv.append(remote(aqkv.at[1:3], kv.at[:, y, TV:TT], y_peer(k)))
    for k in (2, 1, 3):
        r_q.append(remote(vqkv.at[0], q.at[xv], x_peer(k)))
        r_q.append(remote(aqkv.at[0], q.at[xa], x_peer(k)))

    def ordered(rows, base, store):
        count_rows = 64 if rows is not None else HD
        low = low_half(count_rows)

        def tile(n):
            cols = pl.ds(pl.multiple_of(base + 128 * n, 128), 128)
            return (w[rows, cols] if rows is not None else w[:, cols]).astype(F32)

        for p in range(NZ // 2):
            t1, t2 = tile(3 * p + 1), tile(3 * p + 2)
            store(2 * p, tile(3 * p))
            store(2 * p + 1, roll64(jnp.where(low, t2, t1)))
            store(NZ + p, jnp.where(low, t1, t2))

    l_w.wait()

    def store_send(n, value):
        wsend[:, 128 * n : 128 * (n + 1)] = value.astype(BF)

    def store_own(n, value):
        wp[0:HD, 128 * n : 128 * (n + 1)] = value.astype(BF)

    w_rows = pl.ds(pl.multiple_of(core * 64, 64), 64)
    wp_rows = pl.ds(pl.multiple_of(HD + core * 64, 64), 64)
    ordered(w_rows, (1 - x_lo) * HALF, store_send)
    r_w = remote(wsend, wp.at[wp_rows], cross)
    for k in (2, 1, 3):
        r_ga.append(remote(acot_hbm, gb.at[xa], x_peer(k)))
    ordered(None, x_lo * HALF, store_own)

    rate = slope_ref[0] * LOG2E
    key_lane = lax.broadcasted_iota(jnp.int32, (1, QV), 1)
    query_frame_v = (NY * 2 * y + lax.shift_right_logical(key_lane, 6)).astype(F32)
    two = pl.ds(2 * y, 2)
    query_frame_a = frame_ref[two, :].astype(F32)
    qfa = jnp.concatenate([query_frame_a[0:1], query_frame_a[1:2]], axis=1)
    row_v = lax.broadcasted_iota(jnp.int32, (TV, 1), 0)
    for slot in range(NY):
        frame_v = (8 * slot + 2 * xc + lax.shift_right_logical(row_v, 6)).astype(F32)
        bias_v[slot] = rate * jnp.abs(frame_v - qfa)
        one = frame_ref[pl.ds(2 * slot + lax.div(xc, 2), 1), :].astype(F32)
        turned = jnp.broadcast_to(one, (128, 128)).T
        frame_a = jnp.where(core == 1, turned[64:128], turned[0:64])[:, 0:1]
        bias_a[slot] = rate * jnp.abs(frame_a - query_frame_v)

    l_kvv.wait()
    l_kva.wait()
    l_qv.wait()
    l_qa.wait()
    for copy in r_kv + r_q:
        copy.wait_recv()
    c2 = HD ** (-0.5) * LOG2E
    keys = kv[0].reshape(NY * TT, HD)
    values_t = kv[1].reshape(NY * TT, HD).T
    for c in range(3):
        cols = slice(256 * c, 256 * (c + 1))
        scores = (mm(keys, q[cols, :], NT) * c2).reshape(NY, TT, 256)
        part_v, part_a = scores[:, 0:TV], scores[:, TV:TT]
        if c < 2:
            part_a = part_a - bias_a[:, :, cols]
        else:
            part_v = part_v - bias_v[...]
        high = jnp.maximum(
            jnp.max(part_v.reshape(NY * TV, 256), axis=0, keepdims=True),
            jnp.max(part_a.reshape(NY * TA, 256), axis=0, keepdims=True),
        )
        part_v = jnp.exp2(part_v - high)
        part_a = jnp.exp2(part_a - high)
        total = jnp.sum(part_v.reshape(NY * TV, 256), axis=0, keepdims=True) + jnp.sum(
            part_a.reshape(NY * TA, 256), axis=0, keepdims=True
        )
        p_scr[:, 0:TV, cols] = part_v
        p_scr[:, TV:TT, cols] = part_a
        probs = jnp.concatenate([part_v, part_a], axis=1).reshape(NY * TT, 256).astype(BF)
        mixed = mm(values_t, probs).T.astype(BF)
        if c < 2:
            osend[2 * c, 0:TV] = mixed[0:TV]
            osend[2 * c + 1, 0:TV] = mixed[TV:256]
        else:
            for owner in range(NX):
                osend[owner, TV:TT] = mixed[TA * owner : TA * (owner + 1)]
        st_send[0:1, cols] = high
        st_send[1:2, cols] = total
    r_st = [remote(st_send, st_recv.at[k - 1], x_peer(k)) for k in (2, 1, 3)]
    r_o = [remote(osend.at[x_slot(k)], orecv.at[k - 1], x_peer(k)) for k in (2, 1, 3)]

    r_w.wait_recv()
    r_w2 = remote(wp.at[wp_rows], wp.at[wp_rows], sibling)

    for copy in r_st:
        copy.wait_recv()
    highs = [st_send[0:1, :]] + [st_recv[k, 0:1, :] for k in range(3)]
    totals = [st_send[1:2, :]] + [st_recv[k, 1:2, :] for k in range(3)]
    top = jnp.maximum(jnp.maximum(highs[0], highs[1]), jnp.maximum(highs[2], highs[3]))
    scale = [jnp.exp2(h - top) for h in highs]
    norm = sum(t * e for t, e in zip(totals, scale))
    factor = [e / norm for e in scale]
    own_factor = factor[0]
    for k in range(4):
        col_scr[k : k + 1, :] = factor[k]

    turned_v = jnp.concatenate(
        [col_scr[:, xv]] + [jnp.zeros((120, 128), F32)], axis=0
    ).T
    audio_tile = pl.ds(pl.multiple_of(QV + lax.div(xc, 2) * 128, 128), 128)
    turned_a = jnp.concatenate(
        [col_scr[:, audio_tile]] + [jnp.zeros((120, 128), F32)], axis=0
    ).T
    turned_a = jnp.where(core == 1, turned_a[64:128], turned_a[0:64])
    for copy in r_o:
        copy.wait_recv()
    mine = osend[xc].astype(F32)
    mix_v = mine[0:TV] * turned_v[:, 0:1]
    mix_a = mine[TV:TT] * turned_a[:, 0:1]
    for k in range(3):
        other = orecv[k].astype(F32)
        mix_v = mix_v + other[0:TV] * turned_v[:, k + 1 : k + 2]
        mix_a = mix_a + other[TV:TT] * turned_a[:, k + 1 : k + 2]
    mix_vb = mix_v.astype(BF)
    mix_ab = mix_a.astype(BF)
    amix_ref[...] = mix_ab
    mix_own[...] = mix_vb
    r_mix = remote(mix_own, mix_par, cross)

    for copy in r_cot:
        copy.wait_recv()
    low = low_half(64)
    acc = jnp.zeros((TV, 256), F32)
    r_w2.wait_recv()
    for p in range(NZ // 2):
        even, odd = cotb[2 * p], cotb[2 * p + 1]
        lead = jnp.concatenate([even[0:128], odd[0:128]], axis=1)
        acc = acc + mm(lead, wp[:, 256 * p : 256 * (p + 1)], NT)
        be, bo = even[128:192].astype(F32), odd[128:192].astype(F32)
        tails = jnp.concatenate(
            [jnp.where(low, be, roll64(bo)), jnp.where(low, roll64(be), bo)], axis=0
        ).astype(BF)
        acc = acc + mm(tails, wp[:, 1024 + 128 * p : 1024 + 128 * (p + 1)], NT)
    gp_send[...] = acc[:, 128:256].astype(BF)
    r_gp = remote(gp_send, gp_recv, cross)
    l_ga.wait()
    dot_a = jnp.sum(
        jnp.concatenate([gb[xa, :].astype(F32) * mix_ab.astype(F32), jnp.zeros((64, 128), F32)], axis=0).T,
        axis=0,
        keepdims=True,
    )
    r_gp.wait_recv()
    grad = (acc[:, 0:128] + gp_recv[...].astype(F32)).astype(BF)
    g_send[...] = grad
    gb[xv, :] = grad
    r_g = [remote(g_send, gb.at[xv], x_peer(k)) for k in (2, 1, 3)]
    dot_v = jnp.sum((grad.astype(F32) * mix_vb.astype(F32)).T, axis=0, keepdims=True)
    dot_buf[xc, 0:1, 0:128] = dot_v
    dot_buf[xc, 0:1, 128:256] = dot_a
    r_dot = [remote(dot_buf.at[xc], dot_buf.at[xc], x_peer(k)) for k in (2, 1, 3)]

    r_mix.wait_recv()
    both = jnp.concatenate([mix_own[...], mix_par[...]], axis=1)
    for p in range(NZ // 2):
        lead = mm(both, wp[:, 256 * p : 256 * (p + 1)])
        tails = mm(both, wp[:, 1024 + 128 * p : 1024 + 128 * (p + 1)])
        os[2 * p, 0:128] = lead[:, 0:128].astype(BF)
        os[2 * p + 1, 0:128] = lead[:, 128:256].astype(BF)
        upper, lower = tails[0:64], tails[64:128]
        os[2 * p, 128:192] = jnp.where(low, upper, roll64(lower)).astype(BF)
        os[2 * p + 1, 128:192] = jnp.where(low, roll64(upper), lower).astype(BF)
    r_os = [remote(os.at[z_slot(k)], orx.at[k - 1], z_peer(k)) for k in (4, 3, 5, 2, 6, 1, 7)]

    for copy in r_ga + r_g + r_dot:
        copy.wait_recv()
    dots = [dot_buf[k, 0:1, :] for k in range(NX)]
    one_low = low_half(1)
    dot = jnp.concatenate(
        [d[:, 0:128] for d in dots]
        + [
            jnp.where(one_low, dots[0][:, 128:256], roll64(dots[1][:, 128:256])),
            jnp.where(one_low, dots[2][:, 128:256], roll64(dots[3][:, 128:256])),
        ],
        axis=1,
    )
    c = HD ** (-0.5)
    dq_t = jnp.zeros((HD, QT), F32)
    r_dkv = []
    for k in (2, 1, 3, 0):
        slot = lax.rem(y + k, NY)
        key, value = kv[0, slot], kv[1, slot]
        prob = p_scr[slot] * own_factor
        dp = mm(value, gb[...], NT)
        ds = (prob * (dp - dot)).astype(BF)
        dv = mm(prob.astype(BF), gb[...])
        dk = mm(ds, q[...]) * c
        if k:
            dkv_send[k - 1, 0] = dk.astype(BF)
            dkv_send[k - 1, 1] = dv.astype(BF)
            r_dkv.append(remote(dkv_send.at[k - 1], dkv_recv.at[k - 1], y_peer(k)))
        else:
            dkv_own[0] = dk
            dkv_own[1] = dv
        dq_t = dq_t + mm(key.T, ds)
    dq = (dq_t * c).T.astype(BF)
    for owner in range(NX):
        dq_send[owner, 0:TV] = dq[TV * owner : TV * (owner + 1)]
        dq_send[owner, TV:TT] = dq[QV + TA * owner : QV + TA * (owner + 1)]
    r_dq = [remote(dq_send.at[x_slot(k)], dq_recv.at[k - 1], x_peer(k)) for k in (2, 1, 3)]

    for copy in r_os:
        copy.wait_recv()
    total = os[z].astype(F32)
    for k in range(NZ - 1):
        total = total + orx[k].astype(F32)
    out_ref[:, 0:128] = total[0:128].astype(BF)
    packed = total[128:192]
    out_ref[0:64, 128:192] = packed[:, 0:64].astype(BF)
    out_ref[64:128, 128:192] = roll64(packed)[:, 0:64].astype(BF)
    for copy in r_dkv:
        copy.wait_recv()
    dkv = dkv_own[...]
    for k in range(3):
        dkv = dkv + dkv_recv[k].astype(F32)
    dkv = dkv.astype(BF)
    vgrad_ref[1:3] = dkv[:, 0:TV]
    agrad_ref[1:3] = dkv[:, TV:TT]
    for copy in r_dq:
        copy.wait_recv()
    dq = dq_send[xc].astype(F32)
    for k in range(3):
        dq = dq + dq_recv[k].astype(F32)
    dq = dq.astype(BF)
    vgrad_ref[0] = dq[0:TV]
    agrad_ref[0] = dq[TV:TT]
    for copy in sends:
        copy.wait_send()


def per_device(video_qkv, audio_qkv, head_slopes, audio_frame, out_weight, video_cot, audio_cot):
    any_spec = pl.BlockSpec(memory_space=pl.ANY)
    vmem = pl.BlockSpec(memory_space=pltpu.VMEM)
    smem = pl.BlockSpec(memory_space=pltpu.SMEM)
    scratch = [
        pltpu.VMEM((2, NY, TT, HD), BF),
        pltpu.VMEM((QT, HD), BF),
        pltpu.VMEM((QT, HD), BF),
        pltpu.VMEM((NZ, 192, 128), BF),
        pltpu.VMEM((TV, COLS), BF),
        pltpu.VMEM((HD, 2 * HALF), BF),
        pltpu.VMEM((2 * HD, HALF), BF),
        pltpu.VMEM((64, HALF), BF),
        pltpu.VMEM((NY, TV, QA), F32),
        pltpu.VMEM((NY, TA, QV), F32),
        pltpu.VMEM((NY, TT, QT), F32),
        pltpu.VMEM((NX, TT, HD), BF),
        pltpu.VMEM((3, TT, HD), BF),
        pltpu.VMEM((8, QT), F32),
        pltpu.VMEM((3, 8, QT), F32),
        pltpu.VMEM((8, QT), F32),
        pltpu.VMEM((TV, HD), BF),
        pltpu.VMEM((TV, HD), BF),
        pltpu.VMEM((TV, HD), BF),
        pltpu.VMEM((TV, HD), BF),
        pltpu.VMEM((TV, HD), BF),
        pltpu.VMEM((NX, 8, 256), F32),
        pltpu.VMEM((NZ, 192, 128), BF),
        pltpu.VMEM((NZ - 1, 192, 128), BF),
        pltpu.VMEM((3, 2, TT, HD), BF),
        pltpu.VMEM((3, 2, TT, HD), BF),
        pltpu.VMEM((2, TT, HD), F32),
        pltpu.VMEM((NX, TT, HD), BF),
        pltpu.VMEM((3, TT, HD), BF),
        pltpu.SemaphoreType.DMA((8,)),
        pltpu.SemaphoreType.DMA((64,)),
        pltpu.SemaphoreType.DMA((64,)),
    ]
    return pl.pallas_call(
        kernel,
        out_shape=(
            jax.ShapeDtypeStruct((TV, COLS), BF),
            jax.ShapeDtypeStruct((TA, HD), BF),
            jax.ShapeDtypeStruct((3, TV, HD), BF),
            jax.ShapeDtypeStruct((3, TA, HD), BF),
        ),
        in_specs=[any_spec, any_spec, smem, vmem, any_spec, any_spec, any_spec],
        out_specs=(vmem, vmem, vmem, vmem),
        scratch_shapes=scratch,
        compiler_params=pltpu.CompilerParams(
            collective_id=0, has_side_effects=True, vmem_limit_bytes=56 * 1024 * 1024
        ),
    )(
        video_qkv,
        audio_qkv,
        head_slopes,
        audio_frame.reshape(8, 128),
        out_weight,
        video_cot,
        audio_cot,
    )


def solution(mesh):
    in_specs = (
        P(None, "seq", "grp"),
        P(None, "seq", "grp"),
        P("grp"),
        P(),
        P("grp", None),
        P("seq", "grp"),
        P("seq", "grp"),
    )
    out_specs = (P("seq", "grp"), P("seq", "grp"), P(None, "seq", "grp"), P(None, "seq", "grp"))
    return jax.shard_map(
        per_device, mesh=mesh, in_specs=in_specs, out_specs=out_specs, check_vma=False
    )
```

time: 272 us -> 48.9 us (0.18)
  the two profiles are of different devices: /device:TPU:16 before, /device:TPU:1 now
where the time goes in v1:
time: 48.9 us; the launch traced here: 48.6 us
  Pallas kernels  42.2 us (86%)
  local copies, waits for them, and re-layouts  5.16 us (11%)
  between operations  1.31 us (3%)
    pallas_call x1, Pallas kernels, per_device(): pl.pallas_call(kernel, out_shape=(jax.ShapeDtypeStruct((TV, COLS), BF), j...  42.2 us
    unnamed x10, local copies, waits for them, and re-layouts  3.56 us
    pallas_call x1, local copies, waits for them, and re-layouts, per_device(): pl.pallas_call(kernel, out_shape=(jax.ShapeDtypeStruct((TV, COLS), BF), j...  1.6 us

profile of v1, /device:TPU:1, one launch (start us, length us, event | category | flops | bytes accessed | tf_op | source)
XLA Modules:
  0.0 48.6 jit_solution(13143222691919227048)
XLA Ops:
  1.3 1.5 %copy.11.cot_hbm = bf16[128,192]{1,0:T(8,128)(2,1)} copy(bf16[128,192]{0,1:T(8,128)(2,1)} %param.12) | data formatting | bytes 98304 | tf_op args[5]
  2.8 42.2 %shard_map.102 = (bf16[128,192]{1,0:T(8,128)(2,1)}, bf16[64,128]{1,0:T(8,128)(2,1)}, bf16[3,128,128]{2,1,0:T(8,128)(2,1)}, bf16[3,64,128]{2,1,0:T(8,128)(2,1)}) custom-call(bf16[3,128,128]{2,1,0:T(8,128)(2,1)} %vqkv.1, bf16[3,64,128]{2,1,0:T(8,128)(2,1)} %aqkv.1, f32[1]{0:T(128)S(6)} %copy.16.slope_ref, s32[8,128]{1,0:T(8,128)} %bitcast.1, ...), custom_call_target="tpu_custom_call" | custom-call | tf_op jit(solution)/shard_map/pallas_call | solution.py:415
  45.0 0.0 copy-start
  45.0 0.0 copy-start.2
  45.0 1.6 %copy.12 = bf16[128,192]{0,1:T(8,128)(2,1)} copy(bf16[128,192]{1,0:T(8,128)(2,1)} %get-tuple-element.4) | data formatting | bytes 98304 | tf_op jit(solution)/shard_map/pallas_call | solution.py:415
  46.6 0.0 copy-done.2
  46.6 0.6 %copy.17 = bf16[64,128]{1,0:T(8,128)(2,1)} copy(bf16[64,128]{1,0:T(8,128)(2,1)S(1)} %copy-done.2) | data formatting | bytes 32768
  47.2 0.0 copy-done
  47.2 0.0 copy-start.1
  47.2 0.6 %copy.18 = bf16[3,128,128]{2,1,0:T(8,128)(2,1)} copy(bf16[3,128,128]{2,1,0:T(8,128)(2,1)S(1)} %copy-done) | data formatting | bytes 196608
  47.9 0.2 copy-done.1
  48.0 0.6 %copy.19 = bf16[3,64,128]{2,1,0:T(8,128)(2,1)} copy(bf16[3,64,128]{2,1,0:T(8,128)(2,1)S(1)} %copy-done.1) | data formatting | bytes 98304
Async XLA Ops:
  45.0 2.2 %copy-start = (bf16[3,128,128]{2,1,0:T(8,128)(2,1)S(1)}, bf16[3,128,128]{2,1,0:T(8,128)(2,1)}, u32[]{:S(2)}) copy-start(bf16[3,128,128]{2,1,0:T(8,128)(2,1)} %get-tuple-element.14) | copy-start | bytes 294916
  45.0 1.6 %copy-start.2 = (bf16[64,128]{1,0:T(8,128)(2,1)S(1)}, bf16[64,128]{1,0:T(8,128)(2,1)}, u32[]{:S(2)}) copy-start(bf16[64,128]{1,0:T(8,128)(2,1)} %get-tuple-element.13) | copy-start | bytes 49156
  47.2 0.8 %copy-start.1 = (bf16[3,64,128]{2,1,0:T(8,128)(2,1)S(1)}, bf16[3,64,128]{2,1,0:T(8,128)(2,1)}, u32[]{:S(2)}) copy-start(bf16[3,64,128]{2,1,0:T(8,128)(2,1)} %get-tuple-element.15) | copy-start | bytes 147460

commit v2 on v1

v2 whole, which is shorter than its diff:
```python
import math

import jax
import jax.numpy as jnp
from jax import lax
from jax.experimental import pallas as pl
from jax.experimental.pallas import tpu as pltpu
from jax.sharding import PartitionSpec as P

BF = jnp.bfloat16
F32 = jnp.float32
HD = 128
TV = 128
TA = 64
TT = TV + TA
NY = 4
NS = 2 * NY
NZ = 8
QV = 2 * TV
QA = 2 * TA
QT = QV + QA
COLS = 192
HALF = NZ * COLS
LOG2E = 1.4426950408889634
AT_V = COLS + TA
AT_A = AT_V + 3 * TV

NN = (((1,), (0,)), ((), ()))
NT = (((1,), (1,)), ((), ()))


def mm(a, b, dims=NN):
    return lax.dot_general(a, b, dims, preferred_element_type=F32)


def roll64(x):
    return pltpu.roll(x, 64, 1)


def low_half(rows):
    return lax.broadcasted_iota(jnp.int32, (rows, 128), 1) < 64


def kernel(
    vqkv, aqkv, slope_ref, frame_ref, w_hbm, cot_hbm, acot_hbm,
    res_ref,
    kv, q, gb, cotb, wp, wpt, bias_v, bias_a, p_scr,
    osend, orecv, st_send, st_recv, col_scr, mix_own, mix_par,
    gp_send, gp_recv, g_send, dot_buf, os, orx, ofar, ofar_recv,
    sib_send, sib_recv, dkv_send, dkv_recv, dkv_own, dq_send, dq_recv,
    lsem, ssem, rsem,
):
    s = lax.axis_index("seq")
    grp = lax.axis_index("grp")
    y = lax.div(s, 4)
    x_hi = lax.div(lax.rem(s, 4), 2)
    core = lax.rem(s, 2)
    x_lo = lax.div(grp, NZ)
    z = lax.rem(grp, NZ)
    sibling = (s + 1 - 2 * core, grp)
    partner = (s + 2 - 4 * x_hi, grp)
    cross = (s, lax.rem(grp + NZ, 2 * NZ))

    def y_slot(k):
        return lax.rem(y + k, NY)

    def y_peer(k):
        return (lax.rem(s + 4 * k, 4 * NY), grp)

    def z_slot(k):
        return lax.rem(z + k, NZ)

    def z_peer(k):
        return (s, x_lo * NZ + z_slot(k))

    sends = []
    count = [0]

    def remote(src, dst, to):
        i = count[0]
        count[0] += 1
        copy = pltpu.make_async_remote_copy(
            src_ref=src,
            dst_ref=dst,
            send_sem=ssem.at[i],
            recv_sem=rsem.at[i],
            device_id=to,
            device_id_type=pl.DeviceIdType.MESH,
        )
        copy.start()
        sends.append(copy)
        return copy

    local_count = [0]

    def local(src, dst):
        i = local_count[0]
        local_count[0] += 1
        copy = pltpu.make_async_copy(src, dst, lsem.at[i])
        copy.start()
        return copy

    barrier = pltpu.get_barrier_semaphore()
    peers = (
        [z_peer(k) for k in range(1, NZ)]
        + [cross, sibling, partner]
        + [y_peer(k) for k in range(1, NY)]
    )
    for peer in peers:
        pl.semaphore_signal(barrier, inc=1, device_id=peer, device_id_type=pl.DeviceIdType.MESH)

    xv = pl.ds(pl.multiple_of(x_hi * TV, TV), TV)
    xa = pl.ds(pl.multiple_of(QV + x_hi * TA, TA), TA)
    zr = pl.ds(pl.multiple_of(z * COLS, 64), COLS)
    own_cols = pl.ds(pl.multiple_of(x_lo * HALF, HALF), HALF)
    other_cols = pl.ds(pl.multiple_of((1 - x_lo) * HALF, HALF), HALF)
    slot_own = NY * core + y
    l_cot = local(cot_hbm, cotb.at[zr])
    l_w = local(w_hbm.at[:, own_cols], wp.at[0:HD])
    l_kvv = local(vqkv.at[1:3], kv.at[:, slot_own, 0:TV])
    l_kva = local(aqkv.at[1:3], kv.at[:, slot_own, TV:TT])
    l_qv = local(vqkv.at[0], q.at[xv])
    l_qa = local(aqkv.at[0], q.at[xa])
    l_ga = local(acot_hbm, gb.at[xa])

    pl.semaphore_wait(barrier, len(peers))

    def send_kv(to):
        return [
            remote(vqkv.at[1:3], kv.at[:, slot_own, 0:TV], to),
            remote(aqkv.at[1:3], kv.at[:, slot_own, TV:TT], to),
        ]

    r_cot = {k: remote(cot_hbm, cotb.at[zr], z_peer(k)) for k in (2, 6)}
    r_kv = {k: send_kv(y_peer(k)) for k in (1, 3, 2)}
    w_rows = pl.ds(pl.multiple_of(core * 64, 64), 64)
    wp_rows = pl.ds(pl.multiple_of(HD + core * 64, 64), 64)
    r_w = remote(w_hbm.at[w_rows, other_cols], wp.at[wp_rows], cross)
    r_q = [remote(vqkv.at[0], q.at[xv], partner), remote(aqkv.at[0], q.at[xa], partner)]
    for k in (3, 5, 1, 7):
        r_cot[k] = remote(cot_hbm, cotb.at[zr], z_peer(k))
    r_sib = send_kv(sibling)
    r_ga = remote(acot_hbm, gb.at[xa], partner)

    rate = slope_ref[0] * LOG2E
    low1 = low_half(1)
    lane = lax.broadcasted_iota(jnp.int32, (1, QV), 1)
    lane_slot = lax.shift_right_logical(lane, 7)
    lane_frame = lax.shift_right_logical(lane, 6) - 2 * lane_slot
    query_frame_v = (8 * y + 4 * lane_slot + 2 * core + lane_frame).astype(F32)
    first = frame_ref[pl.ds(2 * y, 1), :].astype(F32)
    second = frame_ref[pl.ds(2 * y + 1, 1), :].astype(F32)
    query_frame_a = jnp.where(
        core == 0,
        jnp.where(low1, first, roll64(second)),
        jnp.where(low1, roll64(first), second),
    )
    row_frame = lax.shift_right_logical(lax.broadcasted_iota(jnp.int32, (TV, 1), 0), 6)
    for slot in range(NY):
        one = frame_ref[pl.ds(2 * slot + x_hi, 1), :].astype(F32)
        turned = jnp.broadcast_to(one, (128, 128)).T
        for c in range(2):
            frame_v = (8 * slot + 4 * x_hi + 2 * c + row_frame).astype(F32)
            bias_v[NY * c + slot] = rate * jnp.abs(frame_v - query_frame_a)
            frame_a = turned[64 * c : 64 * (c + 1), 0:1]
            bias_a[NY * c + slot] = rate * jnp.abs(frame_a - query_frame_v)

    for k in (1, 3):
        for copy in r_kv[k]:
            copy.wait_recv()
        at = NY * core + y_slot(NY - k)
        r_sib.append(remote(kv.at[:, at], kv.at[:, at], sibling))
    r_far = []
    for k, half in ((2, 0), (6, 1)):
        r_cot[k].wait_recv()
        rows = pl.ds(pl.multiple_of(z_slot(NZ - k) * COLS + half * 96, 32), 96)
        r_far.append(remote(cotb.at[rows], cotb.at[rows], z_peer(k)))
    l_w.wait()
    wpt[:, 0:HD] = wp[0:HD, :].T
    r_w.wait_recv()
    r_w2 = remote(wp.at[wp_rows], wp.at[wp_rows], sibling)
    for copy in r_kv[2]:
        copy.wait_recv()
    at = NY * core + y_slot(2)
    r_sib.append(remote(kv.at[:, at], kv.at[:, at], sibling))

    l_cot.wait()
    for k in (3, 5, 1, 7):
        r_cot[k].wait_recv()
    for copy in r_far:
        copy.wait_recv()
    r_w2.wait_recv()
    cot_all = cotb[...]
    gp_send[...] = mm(wp[HD : 2 * HD, :], cot_all).astype(BF)
    r_gp = remote(gp_send, gp_recv, cross)
    grad_own = mm(wp[0:HD, :], cot_all)

    l_kvv.wait()
    l_kva.wait()
    l_qv.wait()
    l_qa.wait()
    for copy in r_q + r_sib:
        copy.wait_recv()
    c2 = HD ** (-0.5) * LOG2E
    keys = kv[0].reshape(NS * TT, HD)
    values_t = kv[1].reshape(NS * TT, HD).T
    for c, cols in enumerate((slice(0, QV), slice(QV, QT))):
        wide = cols.stop - cols.start
        scores = (mm(keys, q[cols, :], NT) * c2).reshape(NS, TT, wide)
        part_v, part_a = scores[:, 0:TV], scores[:, TV:TT]
        if c == 0:
            part_a = part_a - bias_a[...]
        else:
            part_v = part_v - bias_v[...]
        high = jnp.maximum(
            jnp.max(part_v.reshape(NS * TV, wide), axis=0, keepdims=True),
            jnp.max(part_a.reshape(NS * TA, wide), axis=0, keepdims=True),
        )
        part_v = jnp.exp2(part_v - high)
        part_a = jnp.exp2(part_a - high)
        total = jnp.sum(part_v.reshape(NS * TV, wide), axis=0, keepdims=True) + jnp.sum(
            part_a.reshape(NS * TA, wide), axis=0, keepdims=True
        )
        p_scr[:, 0:TV, cols] = part_v
        p_scr[:, TV:TT, cols] = part_a
        probs = jnp.concatenate([part_v, part_a], axis=1).reshape(NS * TT, wide).astype(BF)
        mixed = mm(values_t, probs).T.astype(BF)
        rows_each = wide // 2
        for owner in range(2):
            piece = mixed[rows_each * owner : rows_each * (owner + 1)]
            if c == 0:
                osend[owner, 0:TV] = piece
            else:
                osend[owner, TV:TT] = piece
        st_send[0:1, cols] = high
        st_send[1:2, cols] = total
    r_st = remote(st_send, st_recv, partner)
    r_o = remote(osend.at[1 - x_hi], orecv, partner)

    r_gp.wait_recv()
    grad_t = (grad_own + gp_recv[...].astype(F32)).astype(BF).astype(F32)
    grad = grad_t.T.astype(BF)
    g_send[...] = grad
    gb[xv, :] = grad
    r_g = remote(g_send, gb.at[xv], partner)
    wpt[:, HD : 2 * HD] = wp[HD : 2 * HD, :].T

    r_st.wait_recv()
    top = jnp.maximum(st_send[0:1, :], st_recv[0:1, :])
    e_own = jnp.exp2(st_send[0:1, :] - top)
    e_other = jnp.exp2(st_recv[0:1, :] - top)
    norm = st_send[1:2, :] * e_own + st_recv[1:2, :] * e_other
    own_factor = e_own / norm
    col_scr[0:1, :] = own_factor
    col_scr[1:2, :] = e_other / norm

    pad = jnp.zeros((120, 128), F32)
    turned_v = jnp.concatenate([col_scr[:, xv], pad], axis=0).T
    turned_a = jnp.concatenate([col_scr[:, QV:QT], pad], axis=0).T
    turned_a = jnp.where(x_hi == 1, turned_a[64:128], turned_a[0:64])
    r_o.wait_recv()
    mine, other = osend[x_hi].astype(F32), orecv[...].astype(F32)
    mix_v = mine[0:TV] * turned_v[:, 0:1] + other[0:TV] * turned_v[:, 1:2]
    mix_a = mine[TV:TT] * turned_a[:, 0:1] + other[TV:TT] * turned_a[:, 1:2]
    mix_vb = mix_v.astype(BF)
    mix_ab = mix_a.astype(BF)
    mix_own[...] = mix_vb
    r_mix = remote(mix_own, mix_par, cross)
    res_ref[COLS : COLS + TA, :] = mix_ab
    l_ga.wait()
    dot_a = jnp.sum(
        jnp.concatenate(
            [gb[xa, :].astype(F32) * mix_ab.astype(F32), jnp.zeros((64, 128), F32)], axis=0
        ).T,
        axis=0,
        keepdims=True,
    )
    dot_v = jnp.sum(grad_t * mix_vb.astype(F32).T, axis=0, keepdims=True)
    dot_buf[x_hi, 0:1, 0:128] = dot_v
    dot_buf[x_hi, 0:1, 128:256] = dot_a
    r_dot = remote(dot_buf.at[x_hi], dot_buf.at[x_hi], partner)

    r_mix.wait_recv()
    both = jnp.concatenate([mix_own[...], mix_par[...]], axis=1)
    os[...] = mm(wpt[...], both, NT).astype(BF).reshape(NZ, COLS, HD)
    r_ofar = [
        remote(os.at[z_slot(4), 96 * half : 96 * (half + 1)], ofar_recv.at[half], z_peer(k))
        for k, half in ((2, 0), (6, 1))
    ]
    r_os = {k: remote(os.at[z_slot(k)], orx.at[k - 1], z_peer(k)) for k in (3, 5, 1, 7)}

    for copy in (r_ga, r_g, r_dot):
        copy.wait_recv()
    dots = [dot_buf[k, 0:1, :] for k in range(2)]
    dot = jnp.concatenate(
        [dots[0][:, 0:128], dots[1][:, 0:128]]
        + [jnp.where(low1, dots[0][:, 128:256], roll64(dots[1][:, 128:256]))],
        axis=1,
    )
    c = HD ** (-0.5)
    dq_t = jnp.zeros((HD, QT), F32)
    r_half, r_dkv = {}, []
    for mine, k in (
        (0, 2), (0, 1), (1, 2), (0, 3), (1, 1), (0, 0), (1, 3), (1, 0),
    ):
        slot = NY * (core if mine else 1 - core) + y_slot(k)
        key, value = kv[0, slot], kv[1, slot]
        prob = p_scr[slot] * own_factor
        dp = mm(value, gb[...], NT)
        ds = (prob * (dp - dot)).astype(BF)
        dv = mm(prob.astype(BF), gb[...])
        dk = mm(ds, q[...]) * c
        dq_t = dq_t + mm(key.T, ds)
        if not mine:
            sib_send[k, 0] = dk.astype(BF)
            sib_send[k, 1] = dv.astype(BF)
            r_half[k] = remote(sib_send.at[k], sib_recv.at[k], sibling)
        elif k:
            r_half[k].wait_recv()
            dkv_send[k - 1, 0] = (dk + sib_recv[k, 0].astype(F32)).astype(BF)
            dkv_send[k - 1, 1] = (dv + sib_recv[k, 1].astype(F32)).astype(BF)
            r_dkv.append(remote(dkv_send.at[k - 1], dkv_recv.at[k - 1], y_peer(k)))
        else:
            dkv_own[0] = dk
            dkv_own[1] = dv
        if (mine, k) == (1, 2):
            for at, half in ((2, 0), (6, 1)):
                r_ofar[half].wait_recv()
                rows = slice(96 * half, 96 * (half + 1))
                share = os[z_slot(at), rows].astype(F32) + ofar_recv[half].astype(F32)
                ofar[half, rows] = share.astype(BF)
                rest = slice(96 * (1 - half), 96 * (2 - half))
                ofar[half, rest] = os[z_slot(at), rest]
                r_os[at] = remote(ofar.at[half], orx.at[at - 1], z_peer(at))
    dq = (dq_t * c).T.astype(BF)
    for owner in range(2):
        dq_send[owner, 0:TV] = dq[TV * owner : TV * (owner + 1)]
        dq_send[owner, TV:TT] = dq[QV + TA * owner : QV + TA * (owner + 1)]
    r_dq = remote(dq_send.at[1 - x_hi], dq_recv, partner)

    total = os[z].astype(F32)
    for k in (3, 5, 1, 7, 2, 6):
        r_os[k].wait_recv()
        total = total + orx[k - 1].astype(F32)
    res_ref[0:COLS, :] = total.astype(BF)
    r_half[0].wait_recv()
    dkv = dkv_own[...] + sib_recv[0].astype(F32)
    for copy in r_dkv:
        copy.wait_recv()
    for k in range(3):
        dkv = dkv + dkv_recv[k].astype(F32)
    dkv = dkv.astype(BF)
    for n in range(2):
        res_ref[AT_V + TV * (n + 1) : AT_V + TV * (n + 2), :] = dkv[n, 0:TV]
        res_ref[AT_A + TA * (n + 1) : AT_A + TA * (n + 2), :] = dkv[n, TV:TT]
    r_dq.wait_recv()
    dq = (dq_send[x_hi].astype(F32) + dq_recv[...].astype(F32)).astype(BF)
    res_ref[AT_V : AT_V + TV, :] = dq[0:TV]
    res_ref[AT_A : AT_A + TA, :] = dq[TV:TT]
    for copy in sends:
        copy.wait_send()


def unpack(res, out_ref, amix_ref, vgrad_ref, agrad_ref):
    out_ref[...] = res[0:COLS, :]
    amix_ref[...] = res[COLS : COLS + TA, :]
    vgrad_ref[...] = res[AT_V:AT_A, :].reshape(3, TV, HD)
    agrad_ref[...] = res[AT_A : AT_A + 3 * TA, :].reshape(3, TA, HD)


def per_device(video_qkv, audio_qkv, head_slopes, audio_frame, out_weight, video_cot, audio_cot):
    any_spec = pl.BlockSpec(memory_space=pl.ANY)
    vmem = pl.BlockSpec(memory_space=pltpu.VMEM)
    smem = pl.BlockSpec(memory_space=pltpu.SMEM)
    scratch = [
        pltpu.VMEM((2, NS, TT, HD), BF),
        pltpu.VMEM((QT, HD), BF),
        pltpu.VMEM((QT, HD), BF),
        pltpu.VMEM((HALF, TV), BF),
        pltpu.VMEM((2 * HD, HALF), BF),
        pltpu.VMEM((HALF, 2 * HD), BF),
        pltpu.VMEM((NS, TV, QA), F32),
        pltpu.VMEM((NS, TA, QV), F32),
        pltpu.VMEM((NS, TT, QT), F32),
        pltpu.VMEM((2, TT, HD), BF),
        pltpu.VMEM((TT, HD), BF),
        pltpu.VMEM((8, QT), F32),
        pltpu.VMEM((8, QT), F32),
        pltpu.VMEM((8, QT), F32),
        pltpu.VMEM((TV, HD), BF),
        pltpu.VMEM((TV, HD), BF),
        pltpu.VMEM((TV, HD), BF),
        pltpu.VMEM((TV, HD), BF),
        pltpu.VMEM((TV, HD), BF),
        pltpu.VMEM((2, 8, 256), F32),
        pltpu.VMEM((NZ, COLS, HD), BF),
        pltpu.VMEM((NZ - 1, COLS, HD), BF),
        pltpu.VMEM((2, COLS, HD), BF),
        pltpu.VMEM((2, COLS // 2, HD), BF),
        pltpu.VMEM((NY, 2, TT, HD), BF),
        pltpu.VMEM((NY, 2, TT, HD), BF),
        pltpu.VMEM((3, 2, TT, HD), BF),
        pltpu.VMEM((3, 2, TT, HD), BF),
        pltpu.VMEM((2, TT, HD), F32),
        pltpu.VMEM((2, TT, HD), BF),
        pltpu.VMEM((TT, HD), BF),
        pltpu.SemaphoreType.DMA((8,)),
        pltpu.SemaphoreType.DMA((48,)),
        pltpu.SemaphoreType.DMA((48,)),
    ]
    res = pl.pallas_call(
        kernel,
        out_shape=jax.ShapeDtypeStruct((AT_A + 3 * TA, HD), BF),
        in_specs=[any_spec, any_spec, smem, vmem, any_spec, any_spec, any_spec],
        out_specs=vmem,
        scratch_shapes=scratch,
        compiler_params=pltpu.CompilerParams(
            collective_id=0, has_side_effects=True, vmem_limit_bytes=56 * 1024 * 1024
        ),
    )(
        video_qkv,
        audio_qkv,
        head_slopes,
        audio_frame.reshape(8, 128),
        out_weight,
        video_cot.T,
        audio_cot,
    )
    out_t, audio_mix, video_grad, audio_grad = pl.pallas_call(
        unpack,
        out_shape=(
            jax.ShapeDtypeStruct((COLS, TV), BF),
            jax.ShapeDtypeStruct((TA, HD), BF),
            jax.ShapeDtypeStruct((3, TV, HD), BF),
            jax.ShapeDtypeStruct((3, TA, HD), BF),
        ),
        in_specs=[vmem],
        out_specs=(vmem,) * 4,
    )(res)
    return out_t.T, audio_mix, video_grad, audio_grad


def solution(mesh):
    in_specs = (
        P(None, "seq", "grp"),
        P(None, "seq", "grp"),
        P("grp"),
        P(),
        P("grp", None),
        P("seq", "grp"),
        P("seq", "grp"),
    )
    out_specs = (P("seq", "grp"), P("seq", "grp"), P(None, "seq", "grp"), P(None, "seq", "grp"))
    return jax.shard_map(
        per_device, mesh=mesh, in_specs=in_specs, out_specs=out_specs, check_vma=False
    )
```

time: 48.9 us -> 44.4 us (0.908)
  local copies, waits for them, and re-layouts: 5.16 us -> 0 us
  Pallas kernels: 42.2 us -> 43 us
    unnamed x10 -> x0, local copies, waits for them, and re-layouts: 3.56 us -> none
    pallas_call x1 -> x0, local copies, waits for them, and re-layouts: 1.6 us -> none  [per_device(): pl.pallas_call(kernel, out_shape=(jax.ShapeDtypeStruct((TV, COLS), BF), j...]
    pallas_call x1 -> x2, Pallas kernels: 42.2 us -> 43 us  [the longest x1 41.4 us: per_device(): pl.pallas_call(kernel, out_shape=jax.ShapeDtypeStruct((AT_A + 3 * TA, HD)...]
where the time goes in v2:
time: 44.4 us; the launch traced here: 44.3 us
  Pallas kernels  43 us (97%)
  between operations  1.29 us (3%)
    pallas_call x1, Pallas kernels, per_device(): pl.pallas_call(kernel, out_shape=jax.ShapeDtypeStruct((AT_A + 3 * TA, HD)...  41.4 us
    pallas_call x1, Pallas kernels, per_device(): pl.pallas_call(unpack, out_shape=(jax.ShapeDtypeStruct((COLS, TV), BF), j...  1.61 us

profile of v2, /device:TPU:1, one launch (start us, length us, event | category | flops | bytes accessed | tf_op | source)
XLA Modules:
  0.0 44.3 jit_solution(660334832166773197)
XLA Ops:
  1.3 41.4 %shard_map.102.res = bf16[832,128]{1,0:T(8,128)(2,1)} custom-call(bf16[3,128,128]{2,1,0:T(8,128)(2,1)} %vqkv.1, bf16[3,64,128]{2,1,0:T(8,128)(2,1)} %aqkv.1, f32[1]{0:T(128)S(6)} %copy.11.slope_ref, s32[8,128]{1,0:T(8,128)} %bitcast.4, bf16[128,3072]{1,0:T(8,128)(2,1)} %w_hbm.1, bf16[192,128]{1,0:T(8,128)(2,1)} %bitcast.3, bf16[64,128]{1,0:T(8,128)(2,1)} %acot_hbm.1), custom_call_target="tpu_custom_call" | custom-call | tf_op jit(solution)/shard_map/pallas_call | solution.py:411
  42.7 1.6 %shard_map.103 = (bf16[192,128]{1,0:T(8,128)(2,1)}, bf16[64,128]{1,0:T(8,128)(2,1)}, bf16[3,128,128]{2,1,0:T(8,128)(2,1)}, bf16[3,64,128]{2,1,0:T(8,128)(2,1)}) custom-call(bf16[832,128]{1,0:T(8,128)(2,1)} %shard_map.102.res), custom_call_target="tpu_custom_call" | custom-call | tf_op jit(solution)/shard_map/pallas_call | solution.py:429

commit v3 on v2

--- a/solution.py
+++ b/solution.py
@@ -45,8 +45,8 @@
     vqkv, aqkv, slope_ref, frame_ref, w_hbm, cot_hbm, acot_hbm,
     res_ref,
     kv, q, gb, cotb, wp, wpt, bias_v, bias_a, p_scr,
-    osend, orecv, st_send, st_recv, col_scr, mix_own, mix_par,
-    gp_send, gp_recv, g_send, dot_buf, os, orx, ofar, ofar_recv,
+    osend, orecv, oc_recv, od_recv, st_send, st_recv, col_scr,
+    gp_send, gp_recv, go_send, go_recv, gd_recv, dot_buf, os, orx, ofar, ofar_recv,
     sib_send, sib_recv, dkv_send, dkv_recv, dkv_own, dq_send, dq_recv,
     lsem, ssem, rsem,
 ):
@@ -60,6 +60,7 @@
     sibling = (s + 1 - 2 * core, grp)
     partner = (s + 2 - 4 * x_hi, grp)
     cross = (s, lax.rem(grp + NZ, 2 * NZ))
+    corner = (s + 2 - 4 * x_hi, lax.rem(grp + NZ, 2 * NZ))
 
     def y_slot(k):
         return lax.rem(y + k, NY)
@@ -103,7 +104,7 @@
     barrier = pltpu.get_barrier_semaphore()
     peers = (
         [z_peer(k) for k in range(1, NZ)]
-        + [cross, sibling, partner]
+        + [cross, corner, sibling, partner]
         + [y_peer(k) for k in range(1, NY)]
     )
     for peer in peers:
@@ -193,7 +194,10 @@
     cot_all = cotb[...]
     gp_send[...] = mm(wp[HD : 2 * HD, :], cot_all).astype(BF)
     r_gp = remote(gp_send, gp_recv, cross)
-    grad_own = mm(wp[0:HD, :], cot_all)
+    r_gd = remote(gp_send, gd_recv, corner)
+    go_send[...] = mm(wp[0:HD, :], cot_all).astype(BF)
+    r_go = remote(go_send, go_recv, partner)
+    wpt[:, HD : 2 * HD] = wp[HD : 2 * HD, :].T
 
     l_kvv.wait()
     l_kva.wait()
@@ -234,38 +238,51 @@
                 osend[owner, TV:TT] = piece
         st_send[0:1, cols] = high
         st_send[1:2, cols] = total
-    r_st = remote(st_send, st_recv, partner)
-    r_o = remote(osend.at[1 - x_hi], orecv, partner)
+    r_st = [remote(st_send, st_recv.at[n], to) for n, to in enumerate((partner, cross, corner))]
+    r_o = [
+        remote(osend.at[1 - x_hi], orecv, partner),
+        remote(osend.at[x_hi, 0:TV], oc_recv, cross),
+        remote(osend.at[1 - x_hi, 0:TV], od_recv, corner),
+    ]
 
     r_gp.wait_recv()
-    grad_t = (grad_own + gp_recv[...].astype(F32)).astype(BF).astype(F32)
-    grad = grad_t.T.astype(BF)
-    g_send[...] = grad
-    gb[xv, :] = grad
-    r_g = remote(g_send, gb.at[xv], partner)
-    wpt[:, HD : 2 * HD] = wp[HD : 2 * HD, :].T
-
-    r_st.wait_recv()
-    top = jnp.maximum(st_send[0:1, :], st_recv[0:1, :])
-    e_own = jnp.exp2(st_send[0:1, :] - top)
-    e_other = jnp.exp2(st_recv[0:1, :] - top)
-    norm = st_send[1:2, :] * e_own + st_recv[1:2, :] * e_other
-    own_factor = e_own / norm
+    grad_t = (go_send[...].astype(F32) + gp_recv[...].astype(F32)).astype(BF).astype(F32)
+    gb[xv, :] = grad_t.T.astype(BF)
+    r_go.wait_recv()
+    r_gd.wait_recv()
+    grad_o = go_recv[...].astype(F32) + gd_recv[...].astype(F32)
+    xv_other = pl.ds(pl.multiple_of((1 - x_hi) * TV, TV), TV)
+    gb[xv_other, :] = grad_o.T.astype(BF)
+
+    for copy in r_st:
+        copy.wait_recv()
+
+    def shares(first, second):
+        top = jnp.maximum(first[0:1, :], second[0:1, :])
+        e_first = jnp.exp2(first[0:1, :] - top)
+        e_second = jnp.exp2(second[0:1, :] - top)
+        norm = first[1:2, :] * e_first + second[1:2, :] * e_second
+        return e_first / norm, e_second / norm
+
+    own_factor, other_factor = shares(st_send, st_recv[0])
     col_scr[0:1, :] = own_factor
-    col_scr[1:2, :] = e_other / norm
+    col_scr[1:2, :] = other_factor
+    cross_factor, corner_factor = shares(st_recv[1], st_recv[2])
+    col_scr[2:3, :] = cross_factor
+    col_scr[3:4, :] = corner_factor
 
     pad = jnp.zeros((120, 128), F32)
     turned_v = jnp.concatenate([col_scr[:, xv], pad], axis=0).T
     turned_a = jnp.concatenate([col_scr[:, QV:QT], pad], axis=0).T
     turned_a = jnp.where(x_hi == 1, turned_a[64:128], turned_a[0:64])
-    r_o.wait_recv()
+    for copy in r_o:
+        copy.wait_recv()
     mine, other = osend[x_hi].astype(F32), orecv[...].astype(F32)
     mix_v = mine[0:TV] * turned_v[:, 0:1] + other[0:TV] * turned_v[:, 1:2]
     mix_a = mine[TV:TT] * turned_a[:, 0:1] + other[TV:TT] * turned_a[:, 1:2]
     mix_vb = mix_v.astype(BF)
     mix_ab = mix_a.astype(BF)
-    mix_own[...] = mix_vb
-    r_mix = remote(mix_own, mix_par, cross)
+    mix_c = oc_recv[...].astype(F32) * turned_v[:, 2:3] + od_recv[...].astype(F32) * turned_v[:, 3:4]
     res_ref[COLS : COLS + TA, :] = mix_ab
     l_ga.wait()
     dot_a = jnp.sum(
@@ -280,8 +297,7 @@
     dot_buf[x_hi, 0:1, 128:256] = dot_a
     r_dot = remote(dot_buf.at[x_hi], dot_buf.at[x_hi], partner)
 
-    r_mix.wait_recv()
-    both = jnp.concatenate([mix_own[...], mix_par[...]], axis=1)
+    both = jnp.concatenate([mix_vb, mix_c.astype(BF)], axis=1)
     os[...] = mm(wpt[...], both, NT).astype(BF).reshape(NZ, COLS, HD)
     r_ofar = [
         remote(os.at[z_slot(4), 96 * half : 96 * (half + 1)], ofar_recv.at[half], z_peer(k))
@@ -289,8 +305,33 @@
     ]
     r_os = {k: remote(os.at[z_slot(k)], orx.at[k - 1], z_peer(k)) for k in (3, 5, 1, 7)}
 
-    for copy in (r_ga, r_g, r_dot):
-        copy.wait_recv()
+    r_ga.wait_recv()
+    order = ((0, 2), (0, 1), (0, 3), (0, 0), (1, 2), (1, 1), (1, 3), (1, 0))
+    r_half, r_dkv = {}, []
+
+    def hand_over(part, mine, k, value):
+        if not mine:
+            sib_send[k, part] = value.astype(BF)
+            r_half[part, k] = remote(sib_send.at[k, part], sib_recv.at[k, part], sibling)
+        elif k:
+            r_half[part, k].wait_recv()
+            dkv_send[k - 1, part] = (value + sib_recv[k, part].astype(F32)).astype(BF)
+            r_dkv.append(
+                remote(dkv_send.at[k - 1, part], dkv_recv.at[k - 1, part], y_peer(k))
+            )
+        else:
+            dkv_own[part] = value
+
+    def slot_of(mine, k):
+        return NY * (core if mine else 1 - core) + y_slot(k)
+
+    for mine, k in order:
+        slot = slot_of(mine, k)
+        prob = p_scr[slot] * own_factor
+        p_scr[slot] = prob
+        hand_over(1, mine, k, mm(prob.astype(BF), gb[...]))
+
+    r_dot.wait_recv()
     dots = [dot_buf[k, 0:1, :] for k in range(2)]
     dot = jnp.concatenate(
         [dots[0][:, 0:128], dots[1][:, 0:128]]
@@ -299,31 +340,13 @@
     )
     c = HD ** (-0.5)
     dq_t = jnp.zeros((HD, QT), F32)
-    r_half, r_dkv = {}, []
-    for mine, k in (
-        (0, 2), (0, 1), (1, 2), (0, 3), (1, 1), (0, 0), (1, 3), (1, 0),
-    ):
-        slot = NY * (core if mine else 1 - core) + y_slot(k)
-        key, value = kv[0, slot], kv[1, slot]
-        prob = p_scr[slot] * own_factor
-        dp = mm(value, gb[...], NT)
-        ds = (prob * (dp - dot)).astype(BF)
-        dv = mm(prob.astype(BF), gb[...])
-        dk = mm(ds, q[...]) * c
-        dq_t = dq_t + mm(key.T, ds)
-        if not mine:
-            sib_send[k, 0] = dk.astype(BF)
-            sib_send[k, 1] = dv.astype(BF)
-            r_half[k] = remote(sib_send.at[k], sib_recv.at[k], sibling)
-        elif k:
-            r_half[k].wait_recv()
-            dkv_send[k - 1, 0] = (dk + sib_recv[k, 0].astype(F32)).astype(BF)
-            dkv_send[k - 1, 1] = (dv + sib_recv[k, 1].astype(F32)).astype(BF)
-            r_dkv.append(remote(dkv_send.at[k - 1], dkv_recv.at[k - 1], y_peer(k)))
-        else:
-            dkv_own[0] = dk
-            dkv_own[1] = dv
-        if (mine, k) == (1, 2):
+    for mine, k in order:
+        slot = slot_of(mine, k)
+        dp = mm(kv[1, slot], gb[...], NT)
+        ds = (p_scr[slot] * (dp - dot)).astype(BF)
+        hand_over(0, mine, k, mm(ds, q[...]) * c)
+        dq_t = dq_t + mm(kv[0, slot].T, ds)
+        if (mine, k) == (0, 0):
             for at, half in ((2, 0), (6, 1)):
                 r_ofar[half].wait_recv()
                 rows = slice(96 * half, 96 * (half + 1))
@@ -343,7 +366,8 @@
         r_os[k].wait_recv()
         total = total + orx[k - 1].astype(F32)
     res_ref[0:COLS, :] = total.astype(BF)
-    r_half[0].wait_recv()
+    r_half[0, 0].wait_recv()
+    r_half[1, 0].wait_recv()
     dkv = dkv_own[...] + sib_recv[0].astype(F32)
     for copy in r_dkv:
         copy.wait_recv()
@@ -384,14 +408,16 @@
         pltpu.VMEM((NS, TT, QT), F32),
         pltpu.VMEM((2, TT, HD), BF),
         pltpu.VMEM((TT, HD), BF),
-        pltpu.VMEM((8, QT), F32),
-        pltpu.VMEM((8, QT), F32),
-        pltpu.VMEM((8, QT), F32),
         pltpu.VMEM((TV, HD), BF),
         pltpu.VMEM((TV, HD), BF),
-        pltpu.VMEM((TV, HD), BF),
-        pltpu.VMEM((TV, HD), BF),
-        pltpu.VMEM((TV, HD), BF),
+        pltpu.VMEM((8, QT), F32),
+        pltpu.VMEM((3, 8, QT), F32),
+        pltpu.VMEM((8, QT), F32),
+        pltpu.VMEM((HD, TV), BF),
+        pltpu.VMEM((HD, TV), BF),
+        pltpu.VMEM((HD, TV), BF),
+        pltpu.VMEM((HD, TV), BF),
+        pltpu.VMEM((HD, TV), BF),
         pltpu.VMEM((2, 8, 256), F32),
         pltpu.VMEM((NZ, COLS, HD), BF),
         pltpu.VMEM((NZ - 1, COLS, HD), BF),
@@ -405,8 +431,8 @@
         pltpu.VMEM((2, TT, HD), BF),
         pltpu.VMEM((TT, HD), BF),
         pltpu.SemaphoreType.DMA((8,)),
-        pltpu.SemaphoreType.DMA((48,)),
-        pltpu.SemaphoreType.DMA((48,)),
+        pltpu.SemaphoreType.DMA((64,)),
+        pltpu.SemaphoreType.DMA((64,)),
     ]
     res = pl.pallas_call(
         kernel,

time: 44.4 us -> 41.9 us (0.944)
  Pallas kernels: 43 us -> 40.5 us
    pallas_call x1, Pallas kernels: 41.4 us -> 38.9 us  [per_device(): pl.pallas_call(kernel, out_shape=jax.ShapeDtypeStruct((AT_A + 3 * TA, HD)...]
where the time goes in v3:
time: 41.9 us; the launch traced here: 41.8 us
  Pallas kernels  40.5 us (97%)
  between operations  1.29 us (3%)
    pallas_call x1, Pallas kernels, per_device(): pl.pallas_call(kernel, out_shape=jax.ShapeDtypeStruct((AT_A + 3 * TA, HD)...  38.9 us
    pallas_call x1, Pallas kernels, per_device(): pl.pallas_call(unpack, out_shape=(jax.ShapeDtypeStruct((COLS, TV), BF), j...  1.61 us

profile of v3, /device:TPU:1, one launch (start us, length us, event | category | flops | bytes accessed | tf_op | source)
XLA Modules:
  0.0 41.8 jit_solution(7796740087028679912)
XLA Ops:
  1.3 38.9 %shard_map.102.res = bf16[832,128]{1,0:T(8,128)(2,1)} custom-call(bf16[3,128,128]{2,1,0:T(8,128)(2,1)} %vqkv.1, bf16[3,64,128]{2,1,0:T(8,128)(2,1)} %aqkv.1, f32[1]{0:T(128)S(6)} %copy.11.slope_ref, s32[8,128]{1,0:T(8,128)} %bitcast.4, bf16[128,3072]{1,0:T(8,128)(2,1)} %w_hbm.1, bf16[192,128]{1,0:T(8,128)(2,1)} %bitcast.3, bf16[64,128]{1,0:T(8,128)(2,1)} %acot_hbm.1), custom_call_target="tpu_custom_call" | custom-call | tf_op jit(solution)/shard_map/pallas_call | solution.py:437
  40.1 1.6 %shard_map.103 = (bf16[192,128]{1,0:T(8,128)(2,1)}, bf16[64,128]{1,0:T(8,128)(2,1)}, bf16[3,128,128]{2,1,0:T(8,128)(2,1)}, bf16[3,64,128]{2,1,0:T(8,128)(2,1)}) custom-call(bf16[832,128]{1,0:T(8,128)(2,1)} %shard_map.102.res), custom_call_target="tpu_custom_call" | custom-call | tf_op jit(solution)/shard_map/pallas_call | solution.py:455

commit v4 on v3

--- a/solution.py
+++ b/solution.py
@@ -45,7 +45,7 @@
     vqkv, aqkv, slope_ref, frame_ref, w_hbm, cot_hbm, acot_hbm,
     res_ref,
     kv, q, gb, cotb, wp, wpt, bias_v, bias_a, p_scr,
-    osend, orecv, oc_recv, od_recv, st_send, st_recv, col_scr,
+    osend, orecv, oc_recv, od_recv, sv_send, sv_recv, sa_send, sa_recv, col_scr,
     gp_send, gp_recv, go_send, go_recv, gd_recv, dot_buf, os, orx, ofar, ofar_recv,
     sib_send, sib_recv, dkv_send, dkv_recv, dkv_own, dq_send, dq_recv,
     lsem, ssem, rsem,
@@ -184,20 +184,6 @@
         copy.wait_recv()
     at = NY * core + y_slot(2)
     r_sib.append(remote(kv.at[:, at], kv.at[:, at], sibling))
-
-    l_cot.wait()
-    for k in (3, 5, 1, 7):
-        r_cot[k].wait_recv()
-    for copy in r_far:
-        copy.wait_recv()
-    r_w2.wait_recv()
-    cot_all = cotb[...]
-    gp_send[...] = mm(wp[HD : 2 * HD, :], cot_all).astype(BF)
-    r_gp = remote(gp_send, gp_recv, cross)
-    r_gd = remote(gp_send, gd_recv, corner)
-    go_send[...] = mm(wp[0:HD, :], cot_all).astype(BF)
-    r_go = remote(go_send, go_recv, partner)
-    wpt[:, HD : 2 * HD] = wp[HD : 2 * HD, :].T
 
     l_kvv.wait()
     l_kva.wait()
@@ -236,14 +222,69 @@
                 osend[owner, 0:TV] = piece
             else:
                 osend[owner, TV:TT] = piece
-        st_send[0:1, cols] = high
-        st_send[1:2, cols] = total
-    r_st = [remote(st_send, st_recv.at[n], to) for n, to in enumerate((partner, cross, corner))]
-    r_o = [
-        remote(osend.at[1 - x_hi], orecv, partner),
-        remote(osend.at[x_hi, 0:TV], oc_recv, cross),
-        remote(osend.at[1 - x_hi, 0:TV], od_recv, corner),
+        if c == 0:
+            sv_send[0:1, :] = high
+            sv_send[1:2, :] = total
+            r_sv = [
+                remote(sv_send, sv_recv.at[n], to) for n, to in enumerate((partner, cross, corner))
+            ]
+            r_o = [
+                remote(osend.at[1 - x_hi, 0:TV], orecv.at[0:TV], partner),
+                remote(osend.at[x_hi, 0:TV], oc_recv, cross),
+                remote(osend.at[1 - x_hi, 0:TV], od_recv, corner),
+            ]
+        else:
+            sa_send[0:1, :] = high
+            sa_send[1:2, :] = total
+            r_sa = remote(sa_send, sa_recv, partner)
+            r_oa = remote(osend.at[1 - x_hi, TV:TT], orecv.at[TV:TT], partner)
+
+    l_cot.wait()
+    for k in (3, 5, 1, 7):
+        r_cot[k].wait_recv()
+    for copy in r_far:
+        copy.wait_recv()
+    r_w2.wait_recv()
+    cot_all = cotb[...]
+    gp_send[...] = mm(wp[HD : 2 * HD, :], cot_all).astype(BF)
+    r_gp = remote(gp_send, gp_recv, cross)
+    r_gd = remote(gp_send, gd_recv, corner)
+    go_send[...] = mm(wp[0:HD, :], cot_all).astype(BF)
+    r_go = remote(go_send, go_recv, partner)
+    wpt[:, HD : 2 * HD] = wp[HD : 2 * HD, :].T
+
+    for copy in r_sv:
+        copy.wait_recv()
+
+    def shares(first, second):
+        top = jnp.maximum(first[0:1, :], second[0:1, :])
+        e_first = jnp.exp2(first[0:1, :] - top)
+        e_second = jnp.exp2(second[0:1, :] - top)
+        norm = first[1:2, :] * e_first + second[1:2, :] * e_second
+        return e_first / norm, e_second / norm
+
+    own_v, other_v = shares(sv_send, sv_recv[0])
+    col_scr[0:1, 0:QV] = own_v
+    col_scr[1:2, 0:QV] = other_v
+    cross_v, corner_v = shares(sv_recv[1], sv_recv[2])
+    col_scr[2:3, 0:QV] = cross_v
+    col_scr[3:4, 0:QV] = corner_v
+
+    pad = jnp.zeros((120, 128), F32)
+    turned_v = jnp.concatenate([col_scr[:, xv], pad], axis=0).T
+    for copy in r_o:
+        copy.wait_recv()
+    mine, other = osend[x_hi, 0:TV].astype(F32), orecv[0:TV].astype(F32)
+    mix_vb = (mine * turned_v[:, 0:1] + other * turned_v[:, 1:2]).astype(BF)
+    mix_c = oc_recv[...].astype(F32) * turned_v[:, 2:3] + od_recv[...].astype(F32) * turned_v[:, 3:4]
+
+    both = jnp.concatenate([mix_vb, mix_c.astype(BF)], axis=1)
+    os[...] = mm(wpt[...], both, NT).astype(BF).reshape(NZ, COLS, HD)
+    r_ofar = [
+        remote(os.at[z_slot(4), 96 * half : 96 * (half + 1)], ofar_recv.at[half], z_peer(k))
+        for k, half in ((2, 0), (6, 1))
     ]
+    r_os = {k: remote(os.at[z_slot(k)], orx.at[k - 1], z_peer(k)) for k in (3, 5, 1, 7)}
 
     r_gp.wait_recv()
     grad_t = (go_send[...].astype(F32) + gp_recv[...].astype(F32)).astype(BF).astype(F32)
@@ -254,35 +295,16 @@
     xv_other = pl.ds(pl.multiple_of((1 - x_hi) * TV, TV), TV)
     gb[xv_other, :] = grad_o.T.astype(BF)
 
-    for copy in r_st:
-        copy.wait_recv()
-
-    def shares(first, second):
-        top = jnp.maximum(first[0:1, :], second[0:1, :])
-        e_first = jnp.exp2(first[0:1, :] - top)
-        e_second = jnp.exp2(second[0:1, :] - top)
-        norm = first[1:2, :] * e_first + second[1:2, :] * e_second
-        return e_first / norm, e_second / norm
-
-    own_factor, other_factor = shares(st_send, st_recv[0])
-    col_scr[0:1, :] = own_factor
-    col_scr[1:2, :] = other_factor
-    cross_factor, corner_factor = shares(st_recv[1], st_recv[2])
-    col_scr[2:3, :] = cross_factor
-    col_scr[3:4, :] = corner_factor
-
-    pad = jnp.zeros((120, 128), F32)
-    turned_v = jnp.concatenate([col_scr[:, xv], pad], axis=0).T
+    r_sa.wait_recv()
+    own_a, other_a = shares(sa_send, sa_recv)
+    own_factor = jnp.concatenate([own_v, own_a], axis=1)
+    col_scr[0:1, QV:QT] = own_a
+    col_scr[1:2, QV:QT] = other_a
     turned_a = jnp.concatenate([col_scr[:, QV:QT], pad], axis=0).T
     turned_a = jnp.where(x_hi == 1, turned_a[64:128], turned_a[0:64])
-    for copy in r_o:
-        copy.wait_recv()
-    mine, other = osend[x_hi].astype(F32), orecv[...].astype(F32)
-    mix_v = mine[0:TV] * turned_v[:, 0:1] + other[0:TV] * turned_v[:, 1:2]
-    mix_a = mine[TV:TT] * turned_a[:, 0:1] + other[TV:TT] * turned_a[:, 1:2]
-    mix_vb = mix_v.astype(BF)
-    mix_ab = mix_a.astype(BF)
-    mix_c = oc_recv[...].astype(F32) * turned_v[:, 2:3] + od_recv[...].astype(F32) * turned_v[:, 3:4]
+    r_oa.wait_recv()
+    mine, other = osend[x_hi, TV:TT].astype(F32), orecv[TV:TT].astype(F32)
+    mix_ab = (mine * turned_a[:, 0:1] + other * turned_a[:, 1:2]).astype(BF)
     res_ref[COLS : COLS + TA, :] = mix_ab
     l_ga.wait()
     dot_a = jnp.sum(
@@ -296,14 +318,6 @@
     dot_buf[x_hi, 0:1, 0:128] = dot_v
     dot_buf[x_hi, 0:1, 128:256] = dot_a
     r_dot = remote(dot_buf.at[x_hi], dot_buf.at[x_hi], partner)
-
-    both = jnp.concatenate([mix_vb, mix_c.astype(BF)], axis=1)
-    os[...] = mm(wpt[...], both, NT).astype(BF).reshape(NZ, COLS, HD)
-    r_ofar = [
-        remote(os.at[z_slot(4), 96 * half : 96 * (half + 1)], ofar_recv.at[half], z_peer(k))
-        for k, half in ((2, 0), (6, 1))
-    ]
-    r_os = {k: remote(os.at[z_slot(k)], orx.at[k - 1], z_peer(k)) for k in (3, 5, 1, 7)}
 
     r_ga.wait_recv()
     order = ((0, 2), (0, 1), (0, 3), (0, 0), (1, 2), (1, 1), (1, 3), (1, 0))
@@ -331,6 +345,15 @@
         p_scr[slot] = prob
         hand_over(1, mine, k, mm(prob.astype(BF), gb[...]))
 
+    for at, half in ((2, 0), (6, 1)):
+        r_ofar[half].wait_recv()
+        rows = slice(96 * half, 96 * (half + 1))
+        share = os[z_slot(at), rows].astype(F32) + ofar_recv[half].astype(F32)
+        ofar[half, rows] = share.astype(BF)
+        rest = slice(96 * (1 - half), 96 * (2 - half))
+        ofar[half, rest] = os[z_slot(at), rest]
+        r_os[at] = remote(ofar.at[half], orx.at[at - 1], z_peer(at))
+
     r_dot.wait_recv()
     dots = [dot_buf[k, 0:1, :] for k in range(2)]
     dot = jnp.concatenate(
@@ -346,15 +369,6 @@
         ds = (p_scr[slot] * (dp - dot)).astype(BF)
         hand_over(0, mine, k, mm(ds, q[...]) * c)
         dq_t = dq_t + mm(kv[0, slot].T, ds)
-        if (mine, k) == (0, 0):
-            for at, half in ((2, 0), (6, 1)):
-                r_ofar[half].wait_recv()
-                rows = slice(96 * half, 96 * (half + 1))
-                share = os[z_slot(at), rows].astype(F32) + ofar_recv[half].astype(F32)
-                ofar[half, rows] = share.astype(BF)
-                rest = slice(96 * (1 - half), 96 * (2 - half))
-                ofar[half, rest] = os[z_slot(at), rest]
-                r_os[at] = remote(ofar.at[half], orx.at[at - 1], z_peer(at))
     dq = (dq_t * c).T.astype(BF)
     for owner in range(2):
         dq_send[owner, 0:TV] = dq[TV * owner : TV * (owner + 1)]
@@ -410,8 +424,10 @@
         pltpu.VMEM((TT, HD), BF),
         pltpu.VMEM((TV, HD), BF),
         pltpu.VMEM((TV, HD), BF),
-        pltpu.VMEM((8, QT), F32),
-        pltpu.VMEM((3, 8, QT), F32),
+        pltpu.VMEM((8, QV), F32),
+        pltpu.VMEM((3, 8, QV), F32),
+        pltpu.VMEM((8, QA), F32),
+        pltpu.VMEM((8, QA), F32),
         pltpu.VMEM((8, QT), F32),
         pltpu.VMEM((HD, TV), BF),
         pltpu.VMEM((HD, TV), BF),

time: 41.9 us -> 41.1 us (0.981)
  Pallas kernels: 40.5 us -> 39.7 us
    pallas_call x1, Pallas kernels: 38.9 us -> 38.1 us  [per_device(): pl.pallas_call(kernel, out_shape=jax.ShapeDtypeStruct((AT_A + 3 * TA, HD)...]
where the time goes in v4:
time: 41.1 us; the launch traced here: 41 us
  Pallas kernels  39.7 us (97%)
  between operations  1.29 us (3%)
    pallas_call x1, Pallas kernels, per_device(): pl.pallas_call(kernel, out_shape=jax.ShapeDtypeStruct((AT_A + 3 * TA, HD)...  38.1 us
    pallas_call x1, Pallas kernels, per_device(): pl.pallas_call(unpack, out_shape=(jax.ShapeDtypeStruct((COLS, TV), BF), j...  1.61 us

profile of v4, /device:TPU:1, one launch (start us, length us, event | category | flops | bytes accessed | tf_op | source)
XLA Modules:
  0.0 41.0 jit_solution(14795851832023153680)
XLA Ops:
  1.3 38.1 %shard_map.102.res = bf16[832,128]{1,0:T(8,128)(2,1)} custom-call(bf16[3,128,128]{2,1,0:T(8,128)(2,1)} %vqkv.1, bf16[3,64,128]{2,1,0:T(8,128)(2,1)} %aqkv.1, f32[1]{0:T(128)S(6)} %copy.11.slope_ref, s32[8,128]{1,0:T(8,128)} %bitcast.4, bf16[128,3072]{1,0:T(8,128)(2,1)} %w_hbm.1, bf16[192,128]{1,0:T(8,128)(2,1)} %bitcast.3, bf16[64,128]{1,0:T(8,128)(2,1)} %acot_hbm.1), custom_call_target="tpu_custom_call" | custom-call | tf_op jit(solution)/shard_map/pallas_call | solution.py:453
  39.3 1.6 %shard_map.103 = (bf16[192,128]{1,0:T(8,128)(2,1)}, bf16[64,128]{1,0:T(8,128)(2,1)}, bf16[3,128,128]{2,1,0:T(8,128)(2,1)}, bf16[3,64,128]{2,1,0:T(8,128)(2,1)}) custom-call(bf16[832,128]{1,0:T(8,128)(2,1)} %shard_map.102.res), custom_call_target="tpu_custom_call" | custom-call | tf_op jit(solution)/shard_map/pallas_call | solution.py:471

commit v5 on v4

--- a/solution.py
+++ b/solution.py
@@ -133,7 +133,7 @@
         ]
 
     r_cot = {k: remote(cot_hbm, cotb.at[zr], z_peer(k)) for k in (2, 6)}
-    r_kv = {k: send_kv(y_peer(k)) for k in (1, 3, 2)}
+    r_kv = {k: send_kv(y_peer(k)) for k in (1, 3)}
     w_rows = pl.ds(pl.multiple_of(core * 64, 64), 64)
     wp_rows = pl.ds(pl.multiple_of(HD + core * 64, 64), 64)
     r_w = remote(w_hbm.at[w_rows, other_cols], wp.at[wp_rows], cross)
@@ -166,10 +166,12 @@
             frame_a = turned[64 * c : 64 * (c + 1), 0:1]
             bias_a[NY * c + slot] = rate * jnp.abs(frame_a - query_frame_v)
 
-    for k in (1, 3):
+    r_kv[2] = []
+    for part, k in ((0, 1), (1, 3)):
         for copy in r_kv[k]:
             copy.wait_recv()
         at = NY * core + y_slot(NY - k)
+        r_kv[2].append(remote(kv.at[part, at], kv.at[part, at], y_peer(k)))
         r_sib.append(remote(kv.at[:, at], kv.at[:, at], sibling))
     r_far = []
     for k, half in ((2, 0), (6, 1)):

time: 41.1 us -> 41.7 us (1.015)
  Pallas kernels: 39.7 us -> 40.2 us
    pallas_call x1, Pallas kernels: 38.1 us -> 38.6 us  [per_device(): pl.pallas_call(kernel, out_shape=jax.ShapeDtypeStruct((AT_A + 3 * TA, HD)...]
where the time goes in v5:
time: 41.7 us; the launch traced here: 41.5 us
  Pallas kernels  40.2 us (96%)
  between operations  1.29 us (3%)
    pallas_call x1, Pallas kernels, per_device(): pl.pallas_call(kernel, out_shape=jax.ShapeDtypeStruct((AT_A + 3 * TA, HD)...  38.6 us
    pallas_call x1, Pallas kernels, per_device(): pl.pallas_call(unpack, out_shape=(jax.ShapeDtypeStruct((COLS, TV), BF), j...  1.61 us

profile of v5, /device:TPU:1, one launch (start us, length us, event | category | flops | bytes accessed | tf_op | source)
XLA Modules:
  0.0 41.5 jit_solution(16441335969506288277)
XLA Ops:
  1.3 38.6 %shard_map.102.res = bf16[832,128]{1,0:T(8,128)(2,1)} custom-call(bf16[3,128,128]{2,1,0:T(8,128)(2,1)} %vqkv.1, bf16[3,64,128]{2,1,0:T(8,128)(2,1)} %aqkv.1, f32[1]{0:T(128)S(6)} %copy.11.slope_ref, s32[8,128]{1,0:T(8,128)} %bitcast.4, bf16[128,3072]{1,0:T(8,128)(2,1)} %w_hbm.1, bf16[192,128]{1,0:T(8,128)(2,1)} %bitcast.3, bf16[64,128]{1,0:T(8,128)(2,1)} %acot_hbm.1), custom_call_target="tpu_custom_call" | custom-call | tf_op jit(solution)/shard_map/pallas_call | solution.py:455
  39.9 1.6 %shard_map.103 = (bf16[192,128]{1,0:T(8,128)(2,1)}, bf16[64,128]{1,0:T(8,128)(2,1)}, bf16[3,128,128]{2,1,0:T(8,128)(2,1)}, bf16[3,64,128]{2,1,0:T(8,128)(2,1)}) custom-call(bf16[832,128]{1,0:T(8,128)(2,1)} %shard_map.102.res), custom_call_target="tpu_custom_call" | custom-call | tf_op jit(solution)/shard_map/pallas_call | solution.py:473

commit v6 on v4

--- a/solution.py
+++ b/solution.py
@@ -133,7 +133,7 @@
         ]
 
     r_cot = {k: remote(cot_hbm, cotb.at[zr], z_peer(k)) for k in (2, 6)}
-    r_kv = {k: send_kv(y_peer(k)) for k in (1, 3, 2)}
+    r_kv = {k: send_kv(y_peer(k)) for k in (2, 1, 3)}
     w_rows = pl.ds(pl.multiple_of(core * 64, 64), 64)
     wp_rows = pl.ds(pl.multiple_of(HD + core * 64, 64), 64)
     r_w = remote(w_hbm.at[w_rows, other_cols], wp.at[wp_rows], cross)

time: 41.1 us -> 42.2 us (1.027)
  Pallas kernels: 39.7 us -> 40.7 us
    pallas_call x1, Pallas kernels: 38.1 us -> 39.1 us  [per_device(): pl.pallas_call(kernel, out_shape=jax.ShapeDtypeStruct((AT_A + 3 * TA, HD)...]
where the time goes in v6:
time: 42.2 us; the launch traced here: 42 us
  Pallas kernels  40.7 us (96%)
  between operations  1.29 us (3%)
    pallas_call x1, Pallas kernels, per_device(): pl.pallas_call(kernel, out_shape=jax.ShapeDtypeStruct((AT_A + 3 * TA, HD)...  39.1 us
    pallas_call x1, Pallas kernels, per_device(): pl.pallas_call(unpack, out_shape=(jax.ShapeDtypeStruct((COLS, TV), BF), j...  1.61 us

profile of v6, /device:TPU:1, one launch (start us, length us, event | category | flops | bytes accessed | tf_op | source)
XLA Modules:
  0.0 42.0 jit_solution(5641593240942300037)
XLA Ops:
  1.3 39.1 %shard_map.102.res = bf16[832,128]{1,0:T(8,128)(2,1)} custom-call(bf16[3,128,128]{2,1,0:T(8,128)(2,1)} %vqkv.1, bf16[3,64,128]{2,1,0:T(8,128)(2,1)} %aqkv.1, f32[1]{0:T(128)S(6)} %copy.11.slope_ref, s32[8,128]{1,0:T(8,128)} %bitcast.4, bf16[128,3072]{1,0:T(8,128)(2,1)} %w_hbm.1, bf16[192,128]{1,0:T(8,128)(2,1)} %bitcast.3, bf16[64,128]{1,0:T(8,128)(2,1)} %acot_hbm.1), custom_call_target="tpu_custom_call" | custom-call | tf_op jit(solution)/shard_map/pallas_call | solution.py:453
  40.4 1.6 %shard_map.103 = (bf16[192,128]{1,0:T(8,128)(2,1)}, bf16[64,128]{1,0:T(8,128)(2,1)}, bf16[3,128,128]{2,1,0:T(8,128)(2,1)}, bf16[3,64,128]{2,1,0:T(8,128)(2,1)}) custom-call(bf16[832,128]{1,0:T(8,128)(2,1)} %shard_map.102.res), custom_call_target="tpu_custom_call" | custom-call | tf_op jit(solution)/shard_map/pallas_call | solution.py:471
